TPU v7x, 256 devices: a whole 4x4x8 slice. The times are simulated.
256 devices in a mesh: slab: 64 (over x, y, z_lo, core), pencil: 4 (over z_hi).
Axes of the slice: x: 4, y: 4, z: 8 (z_hi: 4, z_lo: 2; z = z_hi * 2 + z_lo), core: 2. Of those that a mesh axis runs over, the one named last changes fastest.
Arguments:
- volume: bfloat16 [4, 256, 64, 256], P(None, 'slab', 'pencil'), may hold values from -6 to 6
- weight_one: bfloat16 [32, 27, 4], replicated, may hold values from -0.625 to 0.625
- weight_two: bfloat16 [64, 27, 32], replicated, may hold values from -0.21875 to 0.21875
- cotangent: bfloat16 [64, 64, 16, 64], P(None, 'slab', 'pencil'), may hold values from -0.18164062 to 0.18164062
Outputs:
- pooled_two: bfloat16 [64, 64, 16, 64], P(None, 'slab', 'pencil')
- grad_one: float32 [32, 27, 4], replicated
- grad_two: float32 [64, 27, 32], P('pencil')
All inputs are finite; a program needn't handle non-finite values.
Results may differ from a plain program's by a relative error of at most 0.019.
Values may be sent and summed in bfloat16 or wider, within the bound.
A program may use at most 64 MiB of HBM per device.

v0:
```python
import jax
import jax.numpy as jnp
from jax import lax
from jax.sharding import PartitionSpec as P


def padded_2(cells, sides, width):
    for axis, dim in sides:
        count = lax.axis_size(axis)
        ends = count - 1
        head = lax.slice_in_dim(cells, 0, width, axis=dim)
        tail = lax.slice_in_dim(cells, cells.shape[dim] - width, cells.shape[dim], axis=dim)
        cells = jnp.concatenate(
            [
                lax.ppermute(tail, axis, [(i, (i + 1) % count) for i in range(ends)]),
                cells,
                lax.ppermute(head, axis, [((i + 1) % count, i) for i in range(ends)]),
            ],
            axis=dim,
        )
    return cells


def act_fn(value):
    return 0.3 * value + 0.7 * jax.nn.softplus(value)


def slope_fn(value):
    return 0.3 + 0.7 * jax.nn.sigmoid(value)


def pool_fn(field):
    c, x, y, z = field.shape
    return field.reshape(c, x // 2, 2, y // 2, 2, z // 2, 2).mean(axis=(2, 4, 6))


def spread_fn(field):
    wide = jnp.repeat(jnp.repeat(jnp.repeat(field, 2, axis=1), 2, axis=2), 2, axis=3)
    return wide * 0.125


def tap_stack(padded, first):
    xs = padded.shape[1] - 2
    ys = padded.shape[2] - 2
    zs = padded.shape[3] - 2
    pieces = [
        padded[:, first : first + xs, b : b + ys, c : c + zs] for b in range(3) for c in range(3)
    ]
    return jnp.concatenate(pieces, axis=0)


def conv_taps(padded, weight):
    outs = weight.shape[0]
    chans = weight.shape[2]
    total = None
    for first in range(3):
        stack = tap_stack(padded, first)
        part = weight[:, 9 * first : 9 * first + 9, :].reshape(outs, 9 * chans)
        term = jnp.einsum("ok,kxyz->oxyz", part, stack, preferred_element_type=jnp.float32)
        total = term if total is None else total + term
    return total


def kernel_grad(padded, grad):
    outs = grad.shape[0]
    chans = padded.shape[0]
    parts = []
    for first in range(3):
        stack = tap_stack(padded, first)
        term = jnp.einsum("oxyz,kxyz->ok", grad, stack, preferred_element_type=jnp.float32)
        parts.append(term.reshape(outs, 9, chans))
    return jnp.concatenate(parts, axis=1)


def flipped(weight):
    return jnp.flip(weight, axis=1).transpose(2, 1, 0)


def pad_last(field):
    return jnp.pad(field, ((0, 0), (0, 0), (0, 0), (1, 1)))


def per_device(volume, weight_one, weight_two, cotangent):
    padded_in = pad_last(padded_2(volume, (("slab", 1), ("pencil", 2)), 1))
    pre_one = conv_taps(padded_in, weight_one)
    pooled_one = pool_fn(act_fn(pre_one)).astype(jnp.bfloat16)
    padded_two = pad_last(padded_2(pooled_one, (("slab", 1), ("pencil", 2)), 1))
    pre_two = conv_taps(padded_two, weight_two)
    grad_pre_two = (slope_fn(pre_two) * spread_fn(cotangent.astype(jnp.float32))).astype(
        jnp.bfloat16
    )
    grad_padded = pad_last(padded_2(grad_pre_two, (("slab", 1), ("pencil", 2)), 1))
    pooled_two = pool_fn(act_fn(pre_two)).astype(jnp.bfloat16)
    local_two = kernel_grad(padded_two, grad_pre_two)
    share_two = lax.psum_scatter(
        local_two.astype(jnp.bfloat16), "pencil", scatter_dimension=0, tiled=True
    ).astype(jnp.float32)
    grad_two = lax.psum(share_two, "slab")
    grad_pooled = conv_taps(grad_padded, flipped(weight_two))
    grad_pre_one = (slope_fn(pre_one) * spread_fn(grad_pooled)).astype(jnp.bfloat16)
    grad_one = lax.psum(kernel_grad(padded_in, grad_pre_one), ("slab", "pencil"))
    return (pooled_two, grad_one, grad_two)


def solution(mesh):
    in_specs = (P(None, "slab", "pencil", None), P(), P(), P(None, "slab", "pencil", None))
    out_specs = (P(None, "slab", "pencil", None), P(), P("pencil", None, None))
    return jax.shard_map(
        per_device, mesh=mesh, in_specs=in_specs, out_specs=out_specs, check_vma=False
    )
```

profile of v0, /device:TPU:1, one launch (start us, length us, event | category | flops | bytes accessed | tf_op | source)
XLA Modules:
  0.0 518.1 jit_solution(986221214411874455)
XLA Ops:
  7.2 1.0 copy.56
  8.3 5.1 collective-permute-start.1
  13.4 1.9 collective-permute-start
  15.4 0.7 fusion.65
  16.1 1.7 fusion.61
  17.8 0.9 reverse_bitcast_fusion
  19.0 4.7 collective-permute-start.2
  23.7 1.3 collective-permute-start.3
  25.2 5.4 %collective-permute-done.3 = bf16[4,6,1,256]{3,0,2,1:T(4,128)(2,1)S(1)} collective-permute-done((bf16[4,6,1,256]{3,0,2,1:T(4,128)(2,1)S(1)}, bf16[4,6,1,256]{3,0,2,1:T(4,128)(2,1)S(1)}, u32[]{:S(2)}, u32[]{:S(2)}) %collective-permute-start.3) | collective-permute-done | bytes 12320 | tf_op jit(solution)/shard_map/ppermute | solution.py:17
  31.0 1.8 fusion.58
  32.8 1.1 pad_maximum_fusion.7
  33.9 1.0 concatenate.111
  34.9 1.8 fusion.56
  36.8 5.1 concatenate.112
  41.9 1.9 fusion.54
  43.8 3.5 concatenate.114
  47.3 6.0 %fusion.2 = (f32[32,4,16,256]{3,0,2,1:T(8,128)}, f32[4,16,256,32]{2,3,1,0:T(8,128)}) fusion(bf16[36,4,16,256]{3,0,2,1:T(8,128)(2,1)S(1)} %concatenate.114, bf16[32,36]{0,1:T(8,128)(2,1)S(1)} %reshape.98, f32[4,16,256,32]{2,3,1,0:T(8,128)} %fusion.56, f32[4,16,256,32]{2,3,1,0:T(8,128)} %fusion.54), kind=kOutput, calls=%fused_computation.5 | convolution fusion | flops 43515904 | bytes 9570560 | tf_op jit(solution)/shard_map/ok,kxyz->oxyz/dot_general | solution.py:59
  53.3 6.3 %copy.65 = f32[32,4,16,256]{0,3,2,1:T(8,128)} copy(f32[32,4,16,256]{3,0,2,1:T(8,128)} %get-tuple-element.115) | data formatting | bytes 4194304 | tf_op jit(solution)/shard_map/add | solution.py:25
  59.6 9.6 %reduce_sum.21 = f32[32,2,8,128]{0,3,2,1:T(8,128)} reduce(f32[32,2,2,8,2,128,2]{0,6,5,4,3,2,1:T(2,128)} %bitcast.145, f32[]{:T(128)} %constant.8.clone.1), dimensions={2,4,6}, to_apply=%region_0.1 | reduce | flops 458752 | bytes 2359300 | tf_op jit(solution)/shard_map/reduce_sum | solution.py:34
  69.2 1.5 copy.66
  70.8 2.9 collective-permute-start.4
  73.7 1.9 collective-permute-start.5
  75.6 0.6 fusion.60
  76.3 3.0 collective-permute-done.5
  79.3 0.6 pad_maximum_fusion.17
  79.9 5.7 %collective-permute-start.6 = (bf16[32,4,1,128]{3,0,2,1:T(8,128)(2,1)}, bf16[32,4,1,128]{3,0,2,1:T(8,128)(2,1)S(1)}, u32[]{:S(2)}, u32[]{:S(2)}) collective-permute-start(bf16[32,4,1,128]{3,0,2,1:T(8,128)(2,1)} %get-tuple-element.84), channel_id=1, source_target_pairs={{0,1},{1,2},{2,3},{4,5},{5,6},{6,7},{8,9},{9,10},{10,11},{12,13},{... | collective-permute-start | bytes 98312 | tf_op jit(solution)/shard_map/ppermute | solution.py:15
  85.7 1.5 collective-permute-start.7
  87.3 0.9 copy.73
  88.3 0.7 reshape.118
  89.0 0.8 reshape.120
  89.8 0.7 reshape.119
  90.7 0.9 copy.72
  91.6 1.1 select_maximum_fusion.2
  92.8 0.8 pad_maximum_fusion.1
  96.7 1.5 multiply_convert_fusion
  99.8 0.7 fusion.59
  100.5 0.7 copy.81
  101.2 0.7 copy.82
  102.0 0.7 copy.83
  102.7 1.1 copy.70
  104.3 3.2 collective-permute-start.8
  107.5 1.9 collective-permute-start.9
  109.5 0.7 copy.85
  110.2 4.5 collective-permute-done.9
  114.7 0.7 pad_maximum_fusion.13
  115.4 4.8 collective-permute-start.10
  120.2 1.3 collective-permute-start.11
  121.5 1.0 pad_maximum_fusion.4
  122.5 1.5 copy.84
  124.1 2.9 collective-permute-done.11
  127.0 0.8 select_maximum_fusion
  132.2 0.5 fusion.23
  132.7 1.3 copy.76
  134.0 1.4 broadcast_in_dim.21
  135.4 1.5 broadcast_in_dim.22
  136.9 3.9 broadcast_in_dim.23
  140.8 7.2 %copy.77 = f32[32,4,16,256]{3,0,2,1:T(8,128)} copy(f32[32,4,16,256]{0,2,3,1:T(8,128)} %bitcast.146) | data formatting | bytes 4194304 | tf_op jit(solution)/shard_map/mul | solution.py:39
  148.1 2.9 fusion.13
  150.9 0.5 convolution_bitcast_fusion.3
  151.5 0.8 copy-done.1
  152.8 0.5 convolution_bitcast_fusion.5
  153.4 86.7 %psum.14 = f32[32,27,4]{0,2,1:T(4,128)} all-reduce(f32[32,27,4]{0,2,1:T(4,128)S(1)} %pad_maximum_fusion.14), channel_id=1, replica_groups=mesh['slab'=64,'pencil'=4] {'slab','pencil'}, use_global_device_ids=true, to_apply=%region_3.4 | all-reduce | flops 3456 | bytes 27648 | tf_op jit(solution)/shard_map/psum | solution.py:101
  240.1 270.4 %psum.15 = f32[16,27,32]{2,1,0:T(8,128)S(1)} all-reduce(bf16[16,27,32]{2,1,0:T(8,128)(2,1)} %reduce-scatter.2.cloned.1.call-done), channel_id=1, replica_groups=mesh['slab'=64,'pencil'=4] {'slab'}, use_global_device_ids=true, to_apply=%region_5.6 | all-reduce | flops 13824 | bytes 82944 | tf_op jit(solution)/shard_map/psum | solution.py:98
  510.4 0.8 copy.86
  (89 shorter events, 11.0 us)
Async XLA Ops:
  7.2 11.7 %copy-start.3 = (bf16[4,4,16,256]{3,2,1,0:T(8,128)(2,1)S(1)}, bf16[4,4,16,256]{3,2,1,0:T(8,128)(2,1)}, u32[]{:S(2)}) copy-start(bf16[4,4,16,256]{3,2,1,0:T(8,128)(2,1)} %param.4) | copy-start | bytes 393220
  7.2 232.9 %reduce-scatter.2.cloned.1.call-start = ((), (), s32[]{:S(2)}) async-start(), calls=%async_computation.1 | async-start | bytes 655360 | tf_op jit(solution)/shard_map/reduce_scatter | solution.py:95
  8.3 10.7 %collective-permute-start.1 = (bf16[4,1,16,256]{3,0,2,1:T(4,128)(2,1)S(1)}, bf16[4,1,16,256]{3,0,2,1:T(4,128)(2,1)S(1)}, u32[]{:S(2)}, u32[]{:S(2)}) collective-permute-start(bf16[4,1,16,256]{3,0,2,1:T(4,128)(2,1)S(1)} %get-tuple-element.110), channel_id=1, source_target_pairs={{4,0},{8,4},{12,8},{16,12},{20,16},{24,20},{28,24},{32,28},{36,32}... | collective-permute-start | bytes 98312 | tf_op jit(solution)/shard_map/ppermute | solution.py:17
  13.4 5.3 %collective-permute-start = (bf16[4,1,16,256]{3,0,2,1:T(4,128)(2,1)S(1)}, bf16[4,1,16,256]{3,0,2,1:T(4,128)(2,1)S(1)}, u32[]{:S(2)}, u32[]{:S(2)}) collective-permute-start(bf16[4,1,16,256]{3,0,2,1:T(4,128)(2,1)S(1)} %get-tuple-element.111), channel_id=1, source_target_pairs={{0,4},{4,8},{8,12},{12,16},{16,20},{20,24},{24,28},{28,32},{32,36}... | collective-permute-start | bytes 98312 | tf_op jit(solution)/shard_map/ppermute | solution.py:15
  19.0 6.2 %collective-permute-start.2 = (bf16[4,6,1,256]{3,0,2,1:T(4,128)(2,1)S(1)}, bf16[4,6,1,256]{3,0,2,1:T(4,128)(2,1)S(1)}, u32[]{:S(2)}, u32[]{:S(2)}) collective-permute-start(bf16[4,6,1,256]{3,0,2,1:T(4,128)(2,1)S(1)} %get-tuple-element.101), channel_id=1, source_target_pairs={{0,1},{1,2},{2,3},{4,5},{5,6},{6,7},{8,9},{9,10},{10,11},{12,13},{... | collective-permute-start | bytes 36872 | tf_op jit(solution)/shard_map/ppermute | solution.py:15
  23.7 6.9 %collective-permute-start.3 = (bf16[4,6,1,256]{3,0,2,1:T(4,128)(2,1)S(1)}, bf16[4,6,1,256]{3,0,2,1:T(4,128)(2,1)S(1)}, u32[]{:S(2)}, u32[]{:S(2)}) collective-permute-start(bf16[4,6,1,256]{3,0,2,1:T(4,128)(2,1)S(1)} %get-tuple-element.102), channel_id=1, source_target_pairs={{1,0},{2,1},{3,2},{5,4},{6,5},{7,6},{9,8},{10,9},{11,10},{13,12},{... | collective-permute-start | bytes 36872 | tf_op jit(solution)/shard_map/ppermute | solution.py:17
  41.9 1.9 copy-start
  41.9 1.9 copy-start.2
  70.7 16.4 %copy-start.11 = (bf16[64,1,4,64]{3,2,1,0:T(4,128)(2,1)S(1)}, bf16[64,1,4,64]{3,2,1,0:T(4,128)(2,1)}, u32[]{:S(2)}) copy-start(bf16[64,1,4,64]{3,2,1,0:T(4,128)(2,1)} %param.7) | copy-start | bytes 98308
  70.8 5.5 %collective-permute-start.4 = (bf16[32,1,8,128]{3,0,2,1:T(8,128)(2,1)S(1)}, bf16[32,1,8,128]{3,0,2,1:T(8,128)(2,1)S(1)}, u32[]{:S(2)}, u32[]{:S(2)}) collective-permute-start(bf16[32,1,8,128]{3,0,2,1:T(8,128)(2,1)S(1)} %get-tuple-element.106), channel_id=1, source_target_pairs={{0,4},{4,8},{8,12},{12,16},{16,20},{20,24},{24,28},{28,32},{32,36}... | collective-permute-start | bytes 196616 | tf_op jit(solution)/shard_map/ppermute | solution.py:15
  73.7 5.6 %collective-permute-start.5 = (bf16[32,1,8,128]{3,0,2,1:T(8,128)(2,1)S(1)}, bf16[32,1,8,128]{3,0,2,1:T(8,128)(2,1)S(1)}, u32[]{:S(2)}, u32[]{:S(2)}) collective-permute-start(bf16[32,1,8,128]{3,0,2,1:T(8,128)(2,1)S(1)} %get-tuple-element.107), channel_id=1, source_target_pairs={{4,0},{8,4},{12,8},{16,12},{20,16},{24,20},{28,24},{32,28},{36,32}... | collective-permute-start | bytes 196616 | tf_op jit(solution)/shard_map/ppermute | solution.py:17
  79.9 11.7 %collective-permute-start.6 = (bf16[32,4,1,128]{3,0,2,1:T(8,128)(2,1)}, bf16[32,4,1,128]{3,0,2,1:T(8,128)(2,1)S(1)}, u32[]{:S(2)}, u32[]{:S(2)}) collective-permute-start(bf16[32,4,1,128]{3,0,2,1:T(8,128)(2,1)} %get-tuple-element.84), channel_id=1, source_target_pairs={{0,1},{1,2},{2,3},{4,5},{5,6},{6,7},{8,9},{9,10},{10,11},{12,13},{... | collective-permute-start | bytes 98312 | tf_op jit(solution)/shard_map/ppermute | solution.py:15
  85.7 6.0 %collective-permute-start.7 = (bf16[32,4,1,128]{3,0,2,1:T(8,128)(2,1)}, bf16[32,4,1,128]{3,0,2,1:T(8,128)(2,1)}, u32[]{:S(2)}, u32[]{:S(2)}) collective-permute-start(bf16[32,4,1,128]{3,0,2,1:T(8,128)(2,1)} %get-tuple-element.85), channel_id=1, source_target_pairs={{1,0},{2,1},{3,2},{5,4},{6,5},{7,6},{9,8},{10,9},{11,10},{13,12},{... | collective-permute-start | bytes 98312 | tf_op jit(solution)/shard_map/ppermute | solution.py:17
  94.5 0.9 copy-start.4
  94.6 1.1 copy-start.5
  95.8 1.0 copy-start.6
  95.8 1.0 copy-start.10
  104.3 5.9 %collective-permute-start.8 = (bf16[64,1,8,128]{3,0,2,1:T(8,128)(2,1)}, bf16[64,1,8,128]{3,0,2,1:T(8,128)(2,1)S(1)}, u32[]{:S(2)}, u32[]{:S(2)}) collective-permute-start(bf16[64,1,8,128]{3,0,2,1:T(8,128)(2,1)} %get-tuple-element.80), channel_id=1, source_target_pairs={{0,4},{4,8},{8,12},{12,16},{16,20},{20,24},{24,28},{28,32},{32,36}... | collective-permute-start | bytes 393224 | tf_op jit(solution)/shard_map/ppermute | solution.py:15
  107.5 7.2 %collective-permute-start.9 = (bf16[64,1,8,128]{3,0,2,1:T(8,128)(2,1)}, bf16[64,1,8,128]{3,0,2,1:T(8,128)(2,1)S(1)}, u32[]{:S(2)}, u32[]{:S(2)}) collective-permute-start(bf16[64,1,8,128]{3,0,2,1:T(8,128)(2,1)} %get-tuple-element.81), channel_id=1, source_target_pairs={{4,0},{8,4},{12,8},{16,12},{20,16},{24,20},{28,24},{32,28},{36,32}... | collective-permute-start | bytes 393224 | tf_op jit(solution)/shard_map/ppermute | solution.py:17
  115.4 8.7 %collective-permute-start.10 = (bf16[64,4,1,128]{3,0,2,1:T(8,128)(2,1)}, bf16[64,4,1,128]{3,0,2,1:T(8,128)(2,1)S(1)}, u32[]{:S(2)}, u32[]{:S(2)}) collective-permute-start(bf16[64,4,1,128]{3,0,2,1:T(8,128)(2,1)} %get-tuple-element.50), channel_id=1, source_target_pairs={{0,1},{1,2},{2,3},{4,5},{5,6},{6,7},{8,9},{9,10},{10,11},{12,13},{... | collective-permute-start | bytes 196616 | tf_op jit(solution)/shard_map/ppermute | solution.py:15
  120.2 6.8 %collective-permute-start.11 = (bf16[64,4,1,128]{3,0,2,1:T(8,128)(2,1)}, bf16[64,4,1,128]{3,0,2,1:T(8,128)(2,1)S(1)}, u32[]{:S(2)}, u32[]{:S(2)}) collective-permute-start(bf16[64,4,1,128]{3,0,2,1:T(8,128)(2,1)} %get-tuple-element.51), channel_id=1, source_target_pairs={{1,0},{2,1},{3,2},{5,4},{6,5},{7,6},{9,8},{10,9},{11,10},{13,12},{... | collective-permute-start | bytes 196616 | tf_op jit(solution)/shard_map/ppermute | solution.py:17
  129.8 0.8 copy-start.9
  130.6 0.8 copy-start.8
  131.4 0.8 copy-start.7
  150.9 1.3 copy-start.1
Sparse Core Ops, SparseCore 0:
  124.2 38.1 reduce-scatter.1
where the time goes:
time: 524 us; the launch traced here: 518 us
  blocking collectives  357 us (68%)
  local copies, waits for them, and re-layouts  57.4 us (11%)
  starting transfers between devices  36.3 us (7%)
  other arithmetic  20 us (4%)
  matrix products  16.7 us (3%)
  waiting for transfers between devices  15.9 us (3%)
  between operations  14.7 us (3%)
    psum x1, blocking collectives, per_device(): grad_two = lax.psum(share_two, 'slab')  270 us
    psum x1, blocking collectives, per_device(): lax.psum(kernel_grad(padded_in, grad_pre_one), ('slab', 'pencil'))  86.7 us
    ppermute x6, starting transfers between devices, padded_2(): lax.ppermute(tail, axis, [(i, (i + 1) % count) for i in range(ends)])  23.2 us
    ppermute x6, waiting for transfers between devices, padded_2(): lax.ppermute(head, axis, [((i + 1) % count, i) for i in range(ends)])  15.9 us
    dot_general x9, matrix products, conv_taps(): jnp.einsum('ok,kxyz->oxyz', part, stack, preferred_element_type=jnp.float32)  13.6 us
    ppermute x6, starting transfers between devices, padded_2(): lax.ppermute(head, axis, [((i + 1) % count, i) for i in range(ends)])  13 us
  transfers between devices with their start and end apart: 13, of which 4 were waited for; matrix products, arithmetic and copies ran while one was open for 7% of the time, Pallas kernels for 0%

commit v1 on v0

v1 whole, which is shorter than its diff:
```python
import functools

import jax
import jax.numpy as jnp
from jax import lax
from jax.experimental import pallas as pl
from jax.experimental.pallas import tpu as pltpu
from jax.sharding import PartitionSpec as P

MESH = pl.DeviceIdType.MESH
F32 = jnp.float32
BF16 = jnp.bfloat16
SIDES = ((1, 0), (-1, 0), (0, 1), (0, -1), (1, 1), (1, -1), (-1, 1), (-1, -1))


def pick(rows, cols, hit):
    r = lax.broadcasted_iota(jnp.int32, (rows, cols), 0)
    c = lax.broadcasted_iota(jnp.int32, (rows, cols), 1)
    return jnp.where(hit(r, c), 1.0, 0.0).astype(BF16)


def dot(a, b):
    return jnp.dot(a, b, preferred_element_type=F32)


def dot_lanes(a, b):
    return lax.dot_general(a, b, (((1,), (1,)), ((), ())), preferred_element_type=F32)


def split(value, count):
    parts = []
    for _ in range(count):
        part = value.astype(BF16)
        parts.append(part)
        value = value - part.astype(F32)
    return parts


def dot_split(value, b, count=2):
    total = None
    for part in split(value, count):
        term = dot(part, b)
        total = term if total is None else total + term
    return total


def act_slope(pre):
    t = jnp.tanh(0.5 * pre)
    act = 0.3 * pre + 0.7 * (jnp.maximum(pre, 0.0) - jnp.log(0.5 + 0.5 * jnp.abs(t)))
    return act, 0.65 + 0.35 * t


def expand_map(xo, yo):
    def hit(r, j):
        a = (j >> 6) - xo
        b = ((j >> 4) & 3) - yo
        slot = j & 15
        ok = (a >= 0) & (a < 3) & (b >= 0) & (b < 3) & (slot < 12)
        return ok & (r == 36 * a + 12 * b + slot)

    return pick(128, 256, hit)


def kernel(
    stages,
    vol,
    w1f,
    w2a,
    w2b,
    cot,
    p2_out,
    g1_out,
    g2_out,
    V,
    PS,
    GS,
    SL,
    ypack,
    xrecv,
    yrecv,
    crecv,
    dw1,
    dw2,
    rs_send,
    rs_recv,
    ar1,
    ar2,
    halo_send,
    halo_recv,
    sem_rs,
    sem_ar1,
    sem_ar2,
):
    slab = lax.axis_index("slab")
    pencil = lax.axis_index("pencil")
    slabs = lax.axis_size("slab")
    pencils = lax.axis_size("pencil")

    def exists(dx, dy):
        x = slab + dx
        y = pencil + dy
        ok = None
        if dx:
            ok = (x >= 0) & (x < slabs)
        if dy:
            oky = (y >= 0) & (y < pencils)
            ok = oky if ok is None else ok & oky
        return ok

    def place(stage):
        axis, size, stride = stages[stage]
        if axis == "pencil":
            return size, pencil, lambda i: (slab, i)
        me = lax.rem(slab // stride, size)
        return size, me, lambda i: (slab + (i - me) * stride, pencil)

    xrecv[...] = jnp.zeros_like(xrecv)
    yrecv[...] = jnp.zeros_like(yrecv)
    crecv[...] = jnp.zeros_like(crecv)
    for field in (PS, GS):
        edge = field.shape[2:]
        for x in (0, 3):
            field[x] = jnp.zeros(field.shape[1:], BF16)
        for y in (0, 9):
            field[1:3, y] = jnp.zeros((2,) + edge, BF16)

    barrier = pltpu.get_barrier_semaphore()
    arrivals = 0
    for dx, dy in SIDES:
        ok = exists(dx, dy)
        arrivals = arrivals + ok.astype(jnp.int32)

        @pl.when(ok)
        def _():
            pl.semaphore_signal(
                barrier, inc=1, device_id=(slab + dx, pencil + dy), device_id_type=MESH
            )

    for stage in range(len(stages)):
        size, me, device = place(stage)
        arrivals = arrivals + (size - 1)
        for d in range(1, size):
            pl.semaphore_signal(
                barrier, inc=1, device_id=device(lax.rem(me + d, size)), device_id_type=MESH
            )

    edges = pick(32, 256, lambda r, c: c == ((r & 15) << 4) + 15 * (r >> 4))
    packed = dot(edges, vol[...].reshape(256, 256)).astype(BF16)
    ypack[0] = packed[:16]
    ypack[1] = packed[16:]
    pl.semaphore_wait(barrier, arrivals)

    def halo_copy(phase, k, refs):
        dx, dy = SIDES[k]
        src, dst = refs(dx, dy)
        return pltpu.make_async_remote_copy(
            src_ref=src,
            dst_ref=dst,
            send_sem=halo_send.at[phase, k],
            recv_sem=halo_recv.at[phase, k],
            device_id=(slab + dx, pencil + dy),
            device_id_type=MESH,
        )

    def halo_start(phase, refs):
        for k, (dx, dy) in enumerate(SIDES):

            @pl.when(exists(dx, dy))
            def _():
                halo_copy(phase, k, refs).start()

    def halo_wait(phase, refs):
        for k, (dx, dy) in enumerate(SIDES):

            @pl.when(exists(dx, dy))
            def _():
                halo_copy(phase, k, refs).wait_send()

            @pl.when(exists(-dx, -dy))
            def _():
                halo_copy(phase, k, refs).wait_recv()

    def volume_refs(dx, dy):
        if dy == 0:
            return vol.at[:, 3 if dx == 1 else 0], xrecv.at[0 if dx == 1 else 1]
        src = ypack.at[1 if dy == 1 else 0]
        side = 0 if dy == 1 else 1
        if dx == 0:
            return src, yrecv.at[side]
        return src, crecv.at[2 * (0 if dx == 1 else 1) + side]

    def field_refs(field, lo, hi, dx, dy):
        sx = {1: 2, -1: 1, 0: pl.ds(1, 2)}[dx]
        tx = {1: 0, -1: 3, 0: pl.ds(1, 2)}[dx]
        sy = {1: 8, -1: 1, 0: pl.ds(1, 8)}[dy]
        ty = {1: 0, -1: 9, 0: pl.ds(1, 8)}[dy]
        rows = pl.ds(lo, hi - lo)
        return field.at[sx, sy, rows], field.at[tx, ty, rows]

    halo_start(0, volume_refs)

    shift_1 = pick(256, 512, lambda r, c: r == jnp.where(c < 256, c - 1, c - 255))
    shift_2 = pick(128, 256, lambda r, c: r == jnp.where(c < 128, c - 1, c - 127))

    def shifted(block):
        sides = dot(block, shift_1).astype(BF16)
        return jnp.concatenate([sides[:, :256], block, sides[:, 256:]], axis=0)

    def order(r, c):
        slot = r & 15
        return (slot < 12) & (c == ((slot >> 2) << 6) + ((slot & 3) << 4) + (r >> 4))

    def order_edge(r, c):
        slot = r & 15
        return (slot < 12) & (c == ((slot >> 2) << 4) + ((slot & 3) << 2) + (r >> 4))

    to_rows = pick(256, 192, order)
    to_edge = pick(64, 48, order_edge)

    def fill(x, block):
        rows = dot(to_rows, shifted(block.reshape(64, 256))).astype(BF16)
        V[x, 1:17] = rows.reshape(16, 16, 256)

    def edge_rows(block):
        return dot(to_edge, shifted(block)).astype(BF16).reshape(4, 16, 256)

    for x in range(4):
        fill(x + 1, vol[:, x])

    w1e = jnp.concatenate(
        [dot(w1f[...], expand_map(xo, yo)).astype(BF16) for xo in range(2) for yo in range(2)],
        axis=0,
    )

    halo_wait(0, volume_refs)
    fill(0, xrecv[0])
    fill(5, xrecv[1])
    for side, y in ((0, 0), (1, 17)):
        V[1:5, y] = edge_rows(yrecv[side])
        V[0, y] = edge_rows(crecv[side])[3]
        V[5, y] = edge_rows(crecv[2 + side])[0]

    def pairs(r, c):
        return (r >> 1) == (c & 127) + (c >> 7) - 1

    pool_1 = pick(256, 384, pairs)

    def window(x1, y1):
        return V[pl.ds(2 * x1, 4), pl.ds(2 * y1, 4)].reshape(256, 256)

    def first_block(y1, carry):
        for x1 in range(2):
            act, slope = act_slope(dot(w1e, window(x1, y1)))
            SL[x1, y1] = slope
            cells = (act[:32] + act[32:64]) + (act[64:96] + act[96:])
            pooled = (0.125 * dot_split(cells, pool_1)).astype(BF16)
            for c in range(3):
                PS[x1 + 1, y1 + 1, 32 * c : 32 * c + 32] = pooled[:, 128 * c : 128 * c + 128]
        return carry

    lax.fori_loop(0, 8, first_block, 0)

    pooled_refs = functools.partial(field_refs, PS, 32, 64)
    halo_start(1, pooled_refs)

    def spread_edges(field, ch):
        def both(cells):
            count = cells.shape[0]
            sides = dot(cells.reshape(count * ch, 128), shift_2).astype(BF16)
            return sides.reshape(count, ch, 256)

        for x in (0, 3):
            sides = both(field[x, :, ch : 2 * ch])
            field[x, :, 0:ch] = sides[:, :, :128]
            field[x, :, 2 * ch :] = sides[:, :, 128:]
        for y in (0, 9):
            sides = both(field[1:3, y, ch : 2 * ch])
            field[1:3, y, 0:ch] = sides[:, :, :128]
            field[1:3, y, 2 * ch :] = sides[:, :, 128:]

    def taps(field, x, y2):
        depth = 3 * field.shape[2]
        one = field[x, pl.ds(2 * y2, 3)].reshape(depth, 128)
        two = field[x, pl.ds(2 * y2 + 1, 3)].reshape(depth, 128)
        return jnp.concatenate([one, two], axis=1)

    halo_wait(1, pooled_refs)
    spread_edges(PS, 32)

    pool_2 = pick(128, 64, lambda r, c: (r >> 1) == c)
    spread_2 = pick(64, 128, lambda r, c: r == (c >> 1))

    def second_block(y2, carry):
        seeds = 0.125 * dot(cot[y2], spread_2)
        seeds = jnp.concatenate([seeds, seeds], axis=1)
        total = None
        for x1 in range(2):
            pre = None
            for a in range(3):
                term = dot(w2a[a], taps(PS, x1 + a, y2))
                pre = term if pre is None else pre + term
            act, slope = act_slope(pre)
            total = act if total is None else total + act
            grad = (slope * seeds).astype(BF16)
            for yo in range(2):
                cells = grad[:, 128 * yo : 128 * yo + 128]
                sides = dot(cells, shift_2).astype(BF16)
                GS[x1 + 1, 2 * y2 + 1 + yo, 64:128] = cells
                GS[x1 + 1, 2 * y2 + 1 + yo, 0:64] = sides[:, :128]
                GS[x1 + 1, 2 * y2 + 1 + yo, 128:192] = sides[:, 128:]
        total = total[:, :128] + total[:, 128:]
        p2_out[y2] = (0.125 * dot_split(total, pool_2)).astype(BF16)
        return carry

    lax.fori_loop(0, 4, second_block, 0)

    grad_refs = functools.partial(field_refs, GS, 64, 128)
    halo_start(2, grad_refs)

    dw2[...] = jnp.zeros_like(dw2)
    groups = dw2.shape[0]
    share = 64 // groups

    def second_grad(y2, carry):
        for a in range(3):
            term = None
            for x1 in range(2):
                cells = jnp.concatenate(
                    [GS[x1 + 1, 2 * y2 + 1, 64:128], GS[x1 + 1, 2 * y2 + 2, 64:128]], axis=1
                )
                part = dot_lanes(cells, taps(PS, x1 + a, y2))
                term = part if term is None else term + part
            for g in range(groups):
                dw2[g, a] += term[share * g : share * g + share]
        return carry

    lax.fori_loop(0, 4, second_grad, 0)
    rs_send[...] = dw2[...].astype(BF16)

    def stage_copy(stage, src, dst_of, sems, d, incoming):
        size, me, device = place(stage)
        peer = lax.rem(me + d, size)
        slot = peer if incoming else me
        return pltpu.make_async_remote_copy(
            src_ref=src(peer, me),
            dst_ref=dst_of(slot),
            send_sem=sems.at[0, d],
            recv_sem=sems.at[1, slot],
            device_id=device(peer),
            device_id_type=MESH,
        )

    def stage_start(stage, src, dst_of, sems):
        for d in range(1, stages[stage][1]):
            stage_copy(stage, src, dst_of, sems, d, False).start()

    def stage_wait(stage, src, dst_of, sems):
        for d in range(1, stages[stage][1]):
            stage_copy(stage, src, dst_of, sems, d, False).wait_send()
            stage_copy(stage, src, dst_of, sems, d, True).wait_recv()

    def scatter(step):
        step(0, lambda peer, me: rs_send.at[peer], lambda slot: rs_recv.at[slot], sem_rs)

    def gather(step, stage, buffer, sems):
        step(
            stage,
            lambda peer, me: buffer.at[stage, me],
            lambda slot: buffer.at[stage, slot],
            sems.at[stage],
        )

    def total_of(buffer, stage):
        total = buffer[stage, 0]
        for i in range(1, stages[stage][1]):
            total = total + buffer[stage, i]
        return total

    scatter(stage_start)

    halo_wait(2, grad_refs)
    spread_edges(GS, 64)
    spread_1 = pick(128, 256, lambda r, c: r == (c >> 1))
    dw1[...] = jnp.zeros_like(dw1)

    def first_grad(y2, carry):
        for x1 in range(2):
            back = None
            for a in range(3):
                term = dot(w2b[a], taps(GS, x1 + a, y2))
                back = term if back is None else back + term
            for yo in range(2):
                y1 = 2 * y2 + yo
                seed = 0.125 * dot_split(back[:, 128 * yo : 128 * yo + 128], spread_1)
                seed = jnp.concatenate([seed] * 4, axis=0)
                grad = (SL[x1, y1] * seed).astype(BF16)
                dw1[...] += dot_lanes(grad, window(x1, y1))
        return carry

    lax.fori_loop(0, 4, first_grad, 0)

    folded = None
    for i in range(4):
        to_taps = expand_map(i // 2, i % 2)
        for part in split(dw1[32 * i : 32 * i + 32], 3):
            term = dot_lanes(part, to_taps)
            folded = term if folded is None else folded + term

    _, mine, _ = place(0)
    ar1[0, mine] = folded
    gather(stage_start, 0, ar1, sem_ar1)
    scatter(stage_wait)
    total = dw2[mine]
    for d in range(1, groups):
        total = total + rs_recv[lax.rem(mine + d, groups)].astype(F32)
    for stage in range(1, len(stages)):
        _, mine, _ = place(stage)
        ar2[stage, mine] = total
        gather(stage_start, stage, ar2, sem_ar2)
        gather(stage_wait, stage - 1, ar1, sem_ar1)
        ar1[stage, mine] = total_of(ar1, stage - 1)
        gather(stage_start, stage, ar1, sem_ar1)
        gather(stage_wait, stage, ar2, sem_ar2)
        total = total_of(ar2, stage)
    g2_out[...] = total
    last = len(stages) - 1
    gather(stage_wait, last, ar1, sem_ar1)
    g1_out[...] = total_of(ar1, last)


def stages_of(mesh):
    stages = [("pencil", mesh.shape["pencil"], 1)]
    stride = 1
    while stride < mesh.shape["slab"]:
        stages.append(("slab", 4, stride))
        stride *= 4
    return stages


def solution(mesh):
    stages = stages_of(mesh)
    pencils = mesh.shape["pencil"]
    share = 64 // pencils
    steps = len(stages)
    most = max(size for _, size, _ in stages)

    def per_device(volume, weight_one, weight_two, cotangent):
        w1f = jnp.pad(weight_one.reshape(32, 108), ((0, 0), (0, 20)))
        w2a = weight_two.reshape(64, 3, 288).transpose(1, 0, 2)
        w2b = jnp.flip(weight_two, axis=1).transpose(2, 1, 0).reshape(32, 3, 576)
        w2b = w2b.transpose(1, 0, 2)
        cot = cotangent.reshape(64, 4, 64).transpose(1, 0, 2)
        vmem = pl.BlockSpec(memory_space=pltpu.VMEM)
        pooled, grad_one, grad_two = pl.pallas_call(
            functools.partial(kernel, stages),
            out_shape=(
                jax.ShapeDtypeStruct((4, 64, 64), BF16),
                jax.ShapeDtypeStruct((32, 128), F32),
                jax.ShapeDtypeStruct((3, share, 288), F32),
            ),
            in_specs=[vmem] * 5,
            out_specs=(vmem,) * 3,
            scratch_shapes=[
                pltpu.VMEM((6, 18, 16, 256), BF16),
                pltpu.VMEM((4, 10, 96, 128), BF16),
                pltpu.VMEM((4, 10, 192, 128), BF16),
                pltpu.VMEM((2, 8, 128, 256), F32),
                pltpu.VMEM((2, 16, 256), BF16),
                pltpu.VMEM((2, 4, 16, 256), BF16),
                pltpu.VMEM((2, 16, 256), BF16),
                pltpu.VMEM((4, 16, 256), BF16),
                pltpu.VMEM((128, 256), F32),
                pltpu.VMEM((pencils, 3, share, 288), F32),
                pltpu.VMEM((pencils, 3, share, 288), BF16),
                pltpu.VMEM((pencils, 3, share, 288), BF16),
                pltpu.VMEM((steps, most, 32, 128), F32),
                pltpu.VMEM((steps, most, 3, share, 288), F32),
                pltpu.SemaphoreType.DMA((3, 8)),
                pltpu.SemaphoreType.DMA((3, 8)),
                pltpu.SemaphoreType.DMA((2, most)),
                pltpu.SemaphoreType.DMA((steps, 2, most)),
                pltpu.SemaphoreType.DMA((steps, 2, most)),
            ],
            compiler_params=pltpu.CompilerParams(
                collective_id=0, has_side_effects=True, vmem_limit_bytes=40 * 2**20
            ),
        )(volume, w1f, w2a, w2b, cot)
        pooled_two = pooled.transpose(1, 0, 2).reshape(64, 1, 4, 64)
        grad_one = grad_one[:, :108].reshape(32, 27, 4)
        grad_two = grad_two.transpose(1, 0, 2).reshape(share, 27, 32)
        return (pooled_two, grad_one, grad_two)

    in_specs = (P(None, "slab", "pencil", None), P(), P(), P(None, "slab", "pencil", None))
    out_specs = (P(None, "slab", "pencil", None), P(), P("pencil", None, None))
    return jax.shard_map(
        per_device, mesh=mesh, in_specs=in_specs, out_specs=out_specs, check_vma=False
    )
```

time: 524 us -> 68.2 us (0.13); the launches traced: 518 us -> 68 us
  blocking collectives: 357 us -> 0 us
  Pallas kernels: 0 us -> 61.6 us
  local copies, waits for them, and re-layouts: 57.4 us -> 5.65 us
  starting transfers between devices: 36.3 us -> 0 us
  other arithmetic: 20 us -> 0 us
  matrix products: 16.7 us -> 0 us
  waiting for transfers between devices: 15.9 us -> 0 us
  between operations: 14.7 us -> 0.72 us
    psum x2 -> x0, blocking collectives: 357 us -> none  [the longest x1 270 us: per_device(): grad_two = lax.psum(share_two, 'slab')]
    pallas_call x0 -> x1, Pallas kernels: none -> 61.6 us  [per_device(): pl.pallas_call(functools.partial(kernel, stages), out_shape=(jax.ShapeDty...]
    ppermute x12 -> x0, starting transfers between devices: 36.3 us -> none  [the longest x6 23.2 us: padded_2(): lax.ppermute(tail, axis, [(i, (i + 1) % count) for i in range(ends)])]
    dot_general x15 -> x0, matrix products: 16.7 us -> none  [the longest x9 13.6 us: conv_taps(): jnp.einsum('ok,kxyz->oxyz', part, stack, preferred_element_type=jnp.float32)]
    ppermute x12 -> x0, waiting for transfers between devices: 15.9 us -> none  [the longest x6 15.9 us: padded_2(): lax.ppermute(head, axis, [((i + 1) % count, i) for i in range(ends)])]
    concatenate x8 -> x0, local copies, waits for them, and re-layouts: 11.9 us -> none  [the longest x6 10.4 us: tap_stack(): return jnp.concatenate(pieces, axis=0)]
    reduce_sum x2 -> x0, other arithmetic: 10.1 us -> none  [pool_fn(): field.reshape(c, x // 2, 2, y // 2, 2, z // 2, 2).mean(axis=(2, 4, 6))]
    mul x4 -> x0, local copies, waits for them, and re-layouts: 9.62 us -> none  [spread_fn(): return wide * 0.125]
  transfers between devices with their start and end apart: 13 -> 0, of which waited for: 4 -> 0; matrix products, arithmetic and copies ran while one was open for 7% -> 0% of each run, Pallas kernels for 0% -> 0%
where the time goes in v1:
time: 68.2 us; the launch traced here: 68 us
  Pallas kernels  61.6 us (90%)
  local copies, waits for them, and re-layouts  5.65 us (8%)
  between operations  0.72 us (1%)
    pallas_call x1, Pallas kernels, per_device(): pl.pallas_call(functools.partial(kernel, stages), out_shape=(jax.ShapeDty...  61.6 us
    unnamed x11, local copies, waits for them, and re-layouts  3.18 us

profile of v1, /device:TPU:1, one launch (start us, length us, event | category | flops | bytes accessed | tf_op | source)
XLA Modules:
  0.0 68.0 jit_solution(18274212279332008393)
XLA Ops:
  0.6 1.0 %reverse_bitcast_fusion = bf16[32,27,64]{2,0,1:T(8,128)(2,1)S(1)} fusion(bf16[64,27,32]{0,2,1:T(8,128)(2,1)} %param.6), kind=kLoop, calls=%fused_computation | loop fusion | bytes 221184 | tf_op jit(solution)/shard_map/transpose | solution.py:450
  1.6 0.1 copy.13
  1.7 0.2 reshape.29
  1.9 0.0 copy-start.1
  1.9 0.9 %copy-done.1 = bf16[64,27,32]{0,2,1:T(8,128)(2,1)S(1)} copy-done((bf16[64,27,32]{0,2,1:T(8,128)(2,1)S(1)}, bf16[64,27,32]{0,2,1:T(8,128)(2,1)}, u32[]{:S(2)}) %copy-start.1) | copy-done | bytes 110616
  2.8 0.0 copy-start.2
  2.8 0.0 copy-start.3
  2.8 0.2 copy.12
  3.0 0.0 copy-start
  3.0 0.6 copy-done.2
  3.7 0.0 copy-done.3
  3.7 0.1 copy.11
  3.8 0.1 copy-done
  3.9 61.6 %shard_map.67 = (bf16[4,64,64]{2,1,0:T(8,128)(2,1)S(1)}, f32[32,128]{1,0:T(8,128)S(1)}, f32[3,16,288]{2,1,0:T(8,128)S(1)}) custom-call(bf16[4,4,16,256]{3,2,1,0:T(8,128)(2,1)S(1)} %copy-done, bf16[32,128]{1,0:T(8,128)(2,1)S(1)} %pad.4.w1f, bf16[3,64,288]{2,1,0:T(8,128)(2,1)S(1)} %bitcast.21, bf16[3,32,576]{2,1,0:T(8,128)(2,1)S(1)} %bitcast.22, ...), custom_call_target="tpu_custom_call" | custom-call | tf_op jit(solution)/shard_map/pallas_call | solution.py:454
  65.6 0.1 reshape.33
  65.8 0.8 %copy.19 = f32[16,27,32]{2,0,1:T(8,128)} copy(f32[16,27,32]{2,1,0:T(8,128)S(1)} %reshape.33) | data formatting | bytes 110592
  66.6 0.1 copy.16
  66.7 0.6 reshape.32
  67.3 0.7 %copy.18 = bf16[64,1,4,64]{3,2,1,0:T(4,128)(2,1)} copy(bf16[64,1,4,64]{3,0,2,1:T(8,128)(2,1)S(1)} %bitcast.25) | data formatting | bytes 65536
  (5 shorter events, 0.1 us)
Async XLA Ops:
  1.9 0.9 %copy-start.1 = (bf16[64,27,32]{0,2,1:T(8,128)(2,1)S(1)}, bf16[64,27,32]{0,2,1:T(8,128)(2,1)}, u32[]{:S(2)}) copy-start(bf16[64,27,32]{0,2,1:T(8,128)(2,1)} %param.6) | copy-start | bytes 331780
  2.8 0.8 %copy-start.2 = (bf16[64,1,4,64]{3,2,1,0:T(4,128)(2,1)S(1)}, bf16[64,1,4,64]{3,2,1,0:T(4,128)(2,1)}, u32[]{:S(2)}) copy-start(bf16[64,1,4,64]{3,2,1,0:T(4,128)(2,1)} %param.7) | copy-start | bytes 98308
  2.8 0.9 %copy-start.3 = (bf16[32,27,4]{0,2,1:T(4,128)(2,1)S(1)}, bf16[32,27,4]{0,2,1:T(4,128)(2,1)}, u32[]{:S(2)}) copy-start(bf16[32,27,4]{0,2,1:T(4,128)(2,1)} %param.5) | copy-start | bytes 20740
  3.0 0.9 %copy-start = (bf16[4,4,16,256]{3,2,1,0:T(8,128)(2,1)S(1)}, bf16[4,4,16,256]{3,2,1,0:T(8,128)(2,1)}, u32[]{:S(2)}) copy-start(bf16[4,4,16,256]{3,2,1,0:T(8,128)(2,1)} %vol.1) | copy-start | bytes 393220

commit v2 on v1

--- a/solution.py
+++ b/solution.py
@@ -8,6 +8,7 @@
 from jax.sharding import PartitionSpec as P
 
 MESH = pl.DeviceIdType.MESH
+LOW = 4
 F32 = jnp.float32
 BF16 = jnp.bfloat16
 SIDES = ((1, 0), (-1, 0), (0, 1), (0, -1), (1, 1), (1, -1), (-1, 1), (-1, -1))
@@ -62,7 +63,6 @@
 
 
 def kernel(
-    stages,
     vol,
     w1f,
     w2a,
@@ -81,15 +81,17 @@
     crecv,
     dw1,
     dw2,
-    rs_send,
-    rs_recv,
-    ar1,
-    ar2,
+    part2,
+    sum_a,
+    sum_b,
+    sum_c,
+    sum_1,
     halo_send,
     halo_recv,
-    sem_rs,
-    sem_ar1,
-    sem_ar2,
+    sem_a,
+    sem_b,
+    sem_c,
+    sem_1,
 ):
     slab = lax.axis_index("slab")
     pencil = lax.axis_index("pencil")
@@ -107,12 +109,10 @@
             ok = oky if ok is None else ok & oky
         return ok
 
-    def place(stage):
-        axis, size, stride = stages[stage]
-        if axis == "pencil":
-            return size, pencil, lambda i: (slab, i)
-        me = lax.rem(slab // stride, size)
-        return size, me, lambda i: (slab + (i - me) * stride, pencil)
+    low = lax.rem(slab, LOW)
+    group_z = (LOW * pencils, low * pencils + pencil, lambda i: (slab - low + i // pencils, lax.rem(i, pencils)))
+    group_xy = (slabs // LOW, slab // LOW, lambda i: (i * LOW + low, pencil))
+    group_low = (LOW, low, lambda i: (slab - low + i, pencil))
 
     xrecv[...] = jnp.zeros_like(xrecv)
     yrecv[...] = jnp.zeros_like(yrecv)
@@ -136,8 +136,7 @@
                 barrier, inc=1, device_id=(slab + dx, pencil + dy), device_id_type=MESH
             )
 
-    for stage in range(len(stages)):
-        size, me, device = place(stage)
+    for size, me, device in (group_z, group_xy):
         arrivals = arrivals + (size - 1)
         for d in range(1, size):
             pl.semaphore_signal(
@@ -148,7 +147,6 @@
     packed = dot(edges, vol[...].reshape(256, 256)).astype(BF16)
     ypack[0] = packed[:16]
     ypack[1] = packed[16:]
-    pl.semaphore_wait(barrier, arrivals)
 
     def halo_copy(phase, k, refs):
         dx, dy = SIDES[k]
@@ -197,8 +195,6 @@
         rows = pl.ds(lo, hi - lo)
         return field.at[sx, sy, rows], field.at[tx, ty, rows]
 
-    halo_start(0, volume_refs)
-
     shift_1 = pick(256, 512, lambda r, c: r == jnp.where(c < 256, c - 1, c - 255))
     shift_2 = pick(128, 256, lambda r, c: r == jnp.where(c < 128, c - 1, c - 127))
 
@@ -232,6 +228,8 @@
         axis=0,
     )
 
+    pl.semaphore_wait(barrier, arrivals)
+    halo_start(0, volume_refs)
     halo_wait(0, volume_refs)
     fill(0, xrecv[0])
     fill(5, xrecv[1])
@@ -335,48 +333,81 @@
         return carry
 
     lax.fori_loop(0, 4, second_grad, 0)
-    rs_send[...] = dw2[...].astype(BF16)
-
-    def stage_copy(stage, src, dst_of, sems, d, incoming):
-        size, me, device = place(stage)
-        peer = lax.rem(me + d, size)
-        slot = peer if incoming else me
-        return pltpu.make_async_remote_copy(
-            src_ref=src(peer, me),
-            dst_ref=dst_of(slot),
-            send_sem=sems.at[0, d],
-            recv_sem=sems.at[1, slot],
-            device_id=device(peer),
-            device_id_type=MESH,
+    part2[...] = dw2[...].astype(BF16)
+
+    def group_copies(group, src_of, dst_of, sems, sends=None, gets=None):
+        size, me, device = group
+
+        def copy(d, slot):
+            peer = lax.rem(me + d, size)
+            return pltpu.make_async_remote_copy(
+                src_ref=src_of(peer),
+                dst_ref=dst_of(peer if slot is None else slot),
+                send_sem=sems.at[0, d],
+                recv_sem=sems.at[1, peer if slot is None else slot],
+                device_id=device(peer),
+                device_id_type=MESH,
+            )
+
+        def each(allowed, act):
+            for d in range(1, size):
+                if allowed is None:
+                    act(d)
+                else:
+                    pl.when(allowed(lax.rem(me + d, size)))(functools.partial(act, d))
+
+        def start():
+            each(sends, lambda d: copy(d, me).start())
+
+        def wait():
+            each(sends, lambda d: copy(d, me).wait_send())
+            each(gets, lambda d: copy(d, None).wait_recv())
+
+        return start, wait
+
+    owner = low < 3
+    mine = jnp.minimum(low, 2)
+    start_a, wait_a = group_copies(
+        group_z,
+        lambda i: part2.at[lax.rem(i, pencils), jnp.minimum(i // pencils, 2)],
+        lambda slot: sum_a.at[slot],
+        sem_a,
+        sends=lambda i: i // pencils < 3,
+        gets=lambda i: owner,
+    )
+    start_b, wait_b = group_copies(
+        group_xy,
+        lambda i: sum_b.at[group_xy[1]],
+        lambda slot: sum_b.at[slot],
+        sem_b,
+        sends=lambda i: owner,
+        gets=lambda i: owner,
+    )
+    start_c, wait_c = group_copies(
+        group_low,
+        lambda i: sum_c.at[low],
+        lambda slot: sum_c.at[slot],
+        sem_c,
+        sends=lambda i: owner,
+        gets=lambda i: i < 3,
+    )
+    sums_1 = [
+        group_copies(
+            group,
+            lambda i, k=k, me=group[1]: sum_1.at[k, me],
+            lambda slot, k=k: sum_1.at[k, slot],
+            sem_1.at[k],
         )
-
-    def stage_start(stage, src, dst_of, sems):
-        for d in range(1, stages[stage][1]):
-            stage_copy(stage, src, dst_of, sems, d, False).start()
-
-    def stage_wait(stage, src, dst_of, sems):
-        for d in range(1, stages[stage][1]):
-            stage_copy(stage, src, dst_of, sems, d, False).wait_send()
-            stage_copy(stage, src, dst_of, sems, d, True).wait_recv()
-
-    def scatter(step):
-        step(0, lambda peer, me: rs_send.at[peer], lambda slot: rs_recv.at[slot], sem_rs)
-
-    def gather(step, stage, buffer, sems):
-        step(
-            stage,
-            lambda peer, me: buffer.at[stage, me],
-            lambda slot: buffer.at[stage, slot],
-            sems.at[stage],
-        )
-
-    def total_of(buffer, stage):
-        total = buffer[stage, 0]
-        for i in range(1, stages[stage][1]):
-            total = total + buffer[stage, i]
+        for k, group in enumerate((group_z, group_xy))
+    ]
+
+    def total_of(slots, size):
+        total = slots[0].astype(F32)
+        for i in range(1, size):
+            total = total + slots[i].astype(F32)
         return total
 
-    scatter(stage_start)
+    start_a()
 
     halo_wait(2, grad_refs)
     spread_edges(GS, 64)
@@ -397,7 +428,16 @@
                 dw1[...] += dot_lanes(grad, window(x1, y1))
         return carry
 
-    lax.fori_loop(0, 4, first_grad, 0)
+    lax.fori_loop(0, 2, first_grad, 0)
+    wait_a()
+
+    @pl.when(owner)
+    def _():
+        sum_a[group_z[1]] = part2[pencil, mine]
+        sum_b[group_xy[1]] = total_of(sum_a, group_z[0]).astype(BF16)
+
+    start_b()
+    lax.fori_loop(2, 4, first_grad, 0)
 
     folded = None
     for i in range(4):
@@ -406,43 +446,31 @@
             term = dot_lanes(part, to_taps)
             folded = term if folded is None else folded + term
 
-    _, mine, _ = place(0)
-    ar1[0, mine] = folded
-    gather(stage_start, 0, ar1, sem_ar1)
-    scatter(stage_wait)
-    total = dw2[mine]
-    for d in range(1, groups):
-        total = total + rs_recv[lax.rem(mine + d, groups)].astype(F32)
-    for stage in range(1, len(stages)):
-        _, mine, _ = place(stage)
-        ar2[stage, mine] = total
-        gather(stage_start, stage, ar2, sem_ar2)
-        gather(stage_wait, stage - 1, ar1, sem_ar1)
-        ar1[stage, mine] = total_of(ar1, stage - 1)
-        gather(stage_start, stage, ar1, sem_ar1)
-        gather(stage_wait, stage, ar2, sem_ar2)
-        total = total_of(ar2, stage)
-    g2_out[...] = total
-    last = len(stages) - 1
-    gather(stage_wait, last, ar1, sem_ar1)
-    g1_out[...] = total_of(ar1, last)
-
-
-def stages_of(mesh):
-    stages = [("pencil", mesh.shape["pencil"], 1)]
-    stride = 1
-    while stride < mesh.shape["slab"]:
-        stages.append(("slab", 4, stride))
-        stride *= 4
-    return stages
+    sum_1[0, group_z[1]] = folded.astype(BF16)
+    sums_1[0][0]()
+    wait_b()
+
+    @pl.when(owner)
+    def _():
+        sum_c[low] = total_of(sum_b, group_xy[0])
+
+    start_c()
+    sums_1[0][1]()
+    sum_1[1, group_xy[1]] = total_of(sum_1.at[0], group_z[0]).astype(BF16)
+    sums_1[1][0]()
+    wait_c()
+    for a in range(3):
+        g2_out[a] = sum_c[a]
+    sums_1[1][1]()
+    g1_out[...] = total_of(sum_1.at[1], group_xy[0])
 
 
 def solution(mesh):
-    stages = stages_of(mesh)
     pencils = mesh.shape["pencil"]
     share = 64 // pencils
-    steps = len(stages)
-    most = max(size for _, size, _ in stages)
+    size_z = LOW * pencils
+    size_xy = mesh.shape["slab"] // LOW
+    most = max(size_z, size_xy)
 
     def per_device(volume, weight_one, weight_two, cotangent):
         w1f = jnp.pad(weight_one.reshape(32, 108), ((0, 0), (0, 20)))
@@ -452,7 +480,7 @@
         cot = cotangent.reshape(64, 4, 64).transpose(1, 0, 2)
         vmem = pl.BlockSpec(memory_space=pltpu.VMEM)
         pooled, grad_one, grad_two = pl.pallas_call(
-            functools.partial(kernel, stages),
+            kernel,
             out_shape=(
                 jax.ShapeDtypeStruct((4, 64, 64), BF16),
                 jax.ShapeDtypeStruct((32, 128), F32),
@@ -472,14 +500,16 @@
                 pltpu.VMEM((128, 256), F32),
                 pltpu.VMEM((pencils, 3, share, 288), F32),
                 pltpu.VMEM((pencils, 3, share, 288), BF16),
-                pltpu.VMEM((pencils, 3, share, 288), BF16),
-                pltpu.VMEM((steps, most, 32, 128), F32),
-                pltpu.VMEM((steps, most, 3, share, 288), F32),
+                pltpu.VMEM((size_z, share, 288), BF16),
+                pltpu.VMEM((size_xy, share, 288), BF16),
+                pltpu.VMEM((LOW, share, 288), F32),
+                pltpu.VMEM((2, most, 32, 128), BF16),
                 pltpu.SemaphoreType.DMA((3, 8)),
                 pltpu.SemaphoreType.DMA((3, 8)),
-                pltpu.SemaphoreType.DMA((2, most)),
-                pltpu.SemaphoreType.DMA((steps, 2, most)),
-                pltpu.SemaphoreType.DMA((steps, 2, most)),
+                pltpu.SemaphoreType.DMA((2, size_z)),
+                pltpu.SemaphoreType.DMA((2, size_xy)),
+                pltpu.SemaphoreType.DMA((2, LOW)),
+                pltpu.SemaphoreType.DMA((2, 2, most)),
             ],
             compiler_params=pltpu.CompilerParams(
                 collective_id=0, has_side_effects=True, vmem_limit_bytes=40 * 2**20

time: 68.2 us -> 64.7 us (0.949)
  Pallas kernels: 61.6 us -> 58.2 us
    pallas_call x1, Pallas kernels: 61.6 us -> 58.2 us  [per_device(): pl.pallas_call(kernel, out_shape=(jax.ShapeDtypeStruct((4, 64, 64), BF16)...]
where the time goes in v2:
time: 64.7 us; the launch traced here: 64.6 us
  Pallas kernels  58.2 us (90%)
  local copies, waits for them, and re-layouts  5.65 us (9%)
  between operations  0.72 us (1%)
    pallas_call x1, Pallas kernels, per_device(): pl.pallas_call(kernel, out_shape=(jax.ShapeDtypeStruct((4, 64, 64), BF16)...  58.2 us
    unnamed x11, local copies, waits for them, and re-layouts  3.18 us

profile of v2, /device:TPU:1, one launch (start us, length us, event | category | flops | bytes accessed | tf_op | source)
XLA Modules:
  0.0 64.6 jit_solution(14540310457808347975)
XLA Ops:
  0.6 1.0 %reverse_bitcast_fusion = bf16[32,27,64]{2,0,1:T(8,128)(2,1)S(1)} fusion(bf16[64,27,32]{0,2,1:T(8,128)(2,1)} %param.6), kind=kLoop, calls=%fused_computation | loop fusion | bytes 221184 | tf_op jit(solution)/shard_map/transpose | solution.py:478
  1.6 0.1 copy.13
  1.7 0.2 reshape.29
  1.9 0.0 copy-start.1
  1.9 0.9 %copy-done.1 = bf16[64,27,32]{0,2,1:T(8,128)(2,1)S(1)} copy-done((bf16[64,27,32]{0,2,1:T(8,128)(2,1)S(1)}, bf16[64,27,32]{0,2,1:T(8,128)(2,1)}, u32[]{:S(2)}) %copy-start.1) | copy-done | bytes 110616
  2.8 0.0 copy-start.2
  2.8 0.0 copy-start.3
  2.8 0.2 copy.12
  3.0 0.0 copy-start
  3.0 0.6 copy-done.2
  3.7 0.0 copy-done.3
  3.7 0.1 copy.11
  3.8 0.1 copy-done
  3.9 58.2 %shard_map.67 = (bf16[4,64,64]{2,1,0:T(8,128)(2,1)S(1)}, f32[32,128]{1,0:T(8,128)S(1)}, f32[3,16,288]{2,1,0:T(8,128)S(1)}) custom-call(bf16[4,4,16,256]{3,2,1,0:T(8,128)(2,1)S(1)} %copy-done, bf16[32,128]{1,0:T(8,128)(2,1)S(1)} %pad.4.w1f, bf16[3,64,288]{2,1,0:T(8,128)(2,1)S(1)} %bitcast.21, bf16[3,32,576]{2,1,0:T(8,128)(2,1)S(1)} %bitcast.22, ...), custom_call_target="tpu_custom_call" | custom-call | tf_op jit(solution)/shard_map/pallas_call | solution.py:482
  62.2 0.1 reshape.33
  62.3 0.8 %copy.19 = f32[16,27,32]{2,0,1:T(8,128)} copy(f32[16,27,32]{2,1,0:T(8,128)S(1)} %reshape.33) | data formatting | bytes 110592
  63.1 0.1 copy.16
  63.2 0.6 reshape.32
  63.9 0.7 %copy.18 = bf16[64,1,4,64]{3,2,1,0:T(4,128)(2,1)} copy(bf16[64,1,4,64]{3,0,2,1:T(8,128)(2,1)S(1)} %bitcast.25) | data formatting | bytes 65536
  (5 shorter events, 0.1 us)
Async XLA Ops:
  1.9 0.9 %copy-start.1 = (bf16[64,27,32]{0,2,1:T(8,128)(2,1)S(1)}, bf16[64,27,32]{0,2,1:T(8,128)(2,1)}, u32[]{:S(2)}) copy-start(bf16[64,27,32]{0,2,1:T(8,128)(2,1)} %param.6) | copy-start | bytes 331780
  2.8 0.8 %copy-start.2 = (bf16[64,1,4,64]{3,2,1,0:T(4,128)(2,1)S(1)}, bf16[64,1,4,64]{3,2,1,0:T(4,128)(2,1)}, u32[]{:S(2)}) copy-start(bf16[64,1,4,64]{3,2,1,0:T(4,128)(2,1)} %param.7) | copy-start | bytes 98308
  2.8 0.9 %copy-start.3 = (bf16[32,27,4]{0,2,1:T(4,128)(2,1)S(1)}, bf16[32,27,4]{0,2,1:T(4,128)(2,1)}, u32[]{:S(2)}) copy-start(bf16[32,27,4]{0,2,1:T(4,128)(2,1)} %param.5) | copy-start | bytes 20740
  3.0 0.9 %copy-start = (bf16[4,4,16,256]{3,2,1,0:T(8,128)(2,1)S(1)}, bf16[4,4,16,256]{3,2,1,0:T(8,128)(2,1)}, u32[]{:S(2)}) copy-start(bf16[4,4,16,256]{3,2,1,0:T(8,128)(2,1)} %vol.1) | copy-start | bytes 393220

commit v3 on v2

v3 whole, which is shorter than its diff:
```python
import functools

import jax
import jax.numpy as jnp
from jax import lax
from jax.experimental import pallas as pl
from jax.experimental.pallas import tpu as pltpu
from jax.sharding import PartitionSpec as P

MESH = pl.DeviceIdType.MESH
LOW = 4
F32 = jnp.float32
BF16 = jnp.bfloat16
SIDES = ((1, 1), (1, -1), (-1, 1), (-1, -1), (1, 0), (-1, 0), (0, 1), (0, -1))


def pick(rows, cols, hit):
    r = lax.broadcasted_iota(jnp.int32, (rows, cols), 0)
    c = lax.broadcasted_iota(jnp.int32, (rows, cols), 1)
    return jnp.where(hit(r, c), 1.0, 0.0).astype(BF16)


def dot(a, b):
    return jnp.dot(a, b, preferred_element_type=F32)


def dot_lanes(a, b):
    return lax.dot_general(a, b, (((1,), (1,)), ((), ())), preferred_element_type=F32)


def split(value, count):
    parts = []
    for _ in range(count):
        part = value.astype(BF16)
        parts.append(part)
        value = value - part.astype(F32)
    return jnp.concatenate(parts, axis=0)


def joined(value, count):
    rows = value.shape[0] // count
    total = value[:rows]
    for i in range(1, count):
        total = total + value[rows * i : rows * i + rows]
    return total


def act_slope(pre):
    t = jnp.tanh(0.5 * pre)
    act = 0.3 * pre + 0.7 * (jnp.maximum(pre, 0.0) - jnp.log(0.5 + 0.5 * jnp.abs(t)))
    return act, 0.65 + 0.35 * t


def expand_map(yo):
    def hit(r, j):
        b = ((j >> 4) & 3) - yo
        slot = j & 15
        return (b >= 0) & (b < 3) & (slot < 12) & (r == 36 * (j >> 6) + 12 * b + slot)

    return pick(128, 192, hit)


def kernel(
    vol_hbm,
    w2_hbm,
    w1f,
    cot,
    p2_out,
    g1_out,
    g2_out,
    vol,
    w2r,
    V,
    PS,
    GS,
    SL,
    CELLS,
    TOT,
    SEED,
    G2,
    BACK,
    W2A,
    W2B,
    MAPS,
    pool_1,
    shift_2,
    spread_1,
    ypack,
    xrecv,
    yrecv,
    crecv,
    dw1,
    dw2,
    part2,
    sum_a,
    sum_b,
    sum_c,
    sum_1,
    sem_in,
    halo_send,
    halo_recv,
    sem_a,
    sem_b,
    sem_c,
    sem_1,
):
    slab = lax.axis_index("slab")
    pencil = lax.axis_index("pencil")
    slabs = lax.axis_size("slab")
    pencils = lax.axis_size("pencil")

    load_vol = pltpu.make_async_copy(vol_hbm, vol, sem_in.at[0])
    load_w2 = pltpu.make_async_copy(w2_hbm, w2r, sem_in.at[1])
    load_vol.start()
    load_w2.start()

    def exists(dx, dy):
        x = slab + dx
        y = pencil + dy
        ok = None
        if dx:
            ok = (x >= 0) & (x < slabs)
        if dy:
            oky = (y >= 0) & (y < pencils)
            ok = oky if ok is None else ok & oky
        return ok

    low = lax.rem(slab, LOW)
    group_z = (
        LOW * pencils,
        low * pencils + pencil,
        lambda i: (slab - low + i // pencils, lax.rem(i, pencils)),
    )
    group_xy = (slabs // LOW, slab // LOW, lambda i: (i * LOW + low, pencil))
    group_low = (LOW, low, lambda i: (slab - low + i, pencil))

    barrier = pltpu.get_barrier_semaphore()
    arrivals = 0
    for dx, dy in SIDES:
        ok = exists(dx, dy)
        arrivals = arrivals + ok.astype(jnp.int32)

        @pl.when(ok)
        def _():
            pl.semaphore_signal(
                barrier, inc=1, device_id=(slab + dx, pencil + dy), device_id_type=MESH
            )

    for size, me, device in (group_z, group_xy):
        arrivals = arrivals + (size - 1)
        for d in range(1, size):
            pl.semaphore_signal(
                barrier, inc=1, device_id=device(lax.rem(me + d, size)), device_id_type=MESH
            )

    def volume_refs(dx, dy):
        if dy == 0:
            return vol.at[:, 3 if dx == 1 else 0], xrecv.at[0 if dx == 1 else 1]
        src = ypack.at[1 if dy == 1 else 0]
        side = 0 if dy == 1 else 1
        if dx == 0:
            return src, yrecv.at[side]
        return src, crecv.at[2 * (0 if dx == 1 else 1) + side]

    def field_refs(field, lo, hi, dx, dy):
        sx = {1: 2, -1: 1, 0: pl.ds(1, 2)}[dx]
        tx = {1: 0, -1: 3, 0: pl.ds(1, 2)}[dx]
        sy = {1: 8, -1: 1, 0: pl.ds(1, 8)}[dy]
        ty = {1: 0, -1: 9, 0: pl.ds(1, 8)}[dy]
        rows = pl.ds(lo, hi - lo)
        return field.at[sx, sy, rows], field.at[tx, ty, rows]

    pooled_refs = functools.partial(field_refs, PS, 32, 64)
    grad_refs = functools.partial(field_refs, GS, 64, 128)

    for dx, dy in SIDES:

        @pl.when(jnp.logical_not(exists(-dx, -dy)))
        def _():
            for refs in (volume_refs, pooled_refs, grad_refs):
                target = refs(dx, dy)[1]
                target[...] = jnp.zeros(target.shape, BF16)

    def halo_copy(phase, k, refs):
        dx, dy = SIDES[k]
        src, dst = refs(dx, dy)
        return pltpu.make_async_remote_copy(
            src_ref=src,
            dst_ref=dst,
            send_sem=halo_send.at[phase, k],
            recv_sem=halo_recv.at[phase, k],
            device_id=(slab + dx, pencil + dy),
            device_id_type=MESH,
        )

    def halo_start(phase, refs):
        for k, (dx, dy) in enumerate(SIDES):

            @pl.when(exists(dx, dy))
            def _():
                halo_copy(phase, k, refs).start()

    def halo_wait(phase, refs):
        for k, (dx, dy) in enumerate(SIDES):

            @pl.when(exists(dx, dy))
            def _():
                halo_copy(phase, k, refs).wait_send()

            @pl.when(exists(-dx, -dy))
            def _():
                halo_copy(phase, k, refs).wait_recv()

    load_vol.wait()
    edges = pick(32, 256, lambda r, c: c == ((r & 15) << 4) + 15 * (r >> 4))
    packed = dot(edges, vol[...].reshape(256, 256)).astype(BF16)
    ypack[0] = packed[:16]
    ypack[1] = packed[16:]

    shift_1 = pick(256, 512, lambda r, c: r == jnp.where(c < 256, c - 1, c - 255))

    def shifted(block):
        sides = dot(block, shift_1).astype(BF16)
        return sides[:, :256], block, sides[:, 256:]

    def order(r, c):
        slot = r & 15
        return (slot < 12) & (c == ((slot >> 2) << 6) + ((slot & 3) << 4) + (r >> 4))

    def order_edge(r, c):
        slot = r & 15
        return (slot < 12) & (c == ((slot >> 2) << 4) + ((slot & 3) << 2) + (r >> 4))

    to_rows = pick(256, 192, order)
    to_edge = pick(64, 48, order_edge)

    def rows_of(parts, lo, hi):
        return jnp.concatenate([part[lo:hi] for part in parts], axis=0)

    local = shifted(jnp.concatenate([vol[:, x].reshape(64, 256) for x in range(4)], axis=0))
    for x in range(4):
        rows = dot(to_rows, rows_of(local, 64 * x, 64 * x + 64)).astype(BF16)
        V[x + 1, 1:17] = rows.reshape(16, 16, 256)

    for yo in range(2):
        MAPS[yo] = expand_map(yo)
    w1p = jnp.concatenate([dot(w1f[...], MAPS[yo]).astype(BF16) for yo in range(2)], axis=0)

    pl.semaphore_wait(barrier, arrivals)
    halo_start(0, volume_refs)

    def window(x, y1):
        return V[pl.ds(x, 3), pl.ds(2 * y1, 4)].reshape(192, 256)

    def first_cells(x, y1):
        act, slope = act_slope(dot(w1p, window(x, y1)))
        SL[x, y1] = slope
        return act[:32] + act[32:]

    def inner(i, carry):
        for x in (1, 2):
            for j in range(2):
                CELLS[x - 1, 1 + 2 * i + j] = first_cells(x, 1 + 2 * i + j)
        return carry

    lax.fori_loop(0, 3, inner, 0)

    def pairs(r, c):
        return (r >> 1) == (c & 127) + (c >> 7) - 1

    pool_1[...] = pick(256, 384, pairs)
    shift_2[...] = pick(128, 256, lambda r, c: r == jnp.where(c < 128, c - 1, c - 127))
    spread_1[...] = pick(128, 256, lambda r, c: r == (c >> 1))

    halo_wait(0, volume_refs)
    arrived = shifted(
        jnp.concatenate(
            [xrecv[s].reshape(64, 256) for s in range(2)]
            + [yrecv[s] for s in range(2)]
            + [crecv[s] for s in range(4)],
            axis=0,
        )
    )
    for side, x in ((0, 0), (1, 5)):
        rows = dot(to_rows, rows_of(arrived, 64 * side, 64 * side + 64)).astype(BF16)
        V[x, 1:17] = rows.reshape(16, 16, 256)
    for side, y in ((0, 0), (1, 17)):
        at = 128 + 16 * side
        V[1:5, y] = dot(to_edge, rows_of(arrived, at, at + 16)).astype(BF16).reshape(4, 16, 256)
        at = 160 + 16 * side
        V[0, y] = dot(to_edge[48:], rows_of(arrived, at, at + 16)).astype(BF16)
        at = 192 + 16 * side
        V[5, y] = dot(to_edge[:16], rows_of(arrived, at, at + 16)).astype(BF16)

    for x in (1, 2):
        for y1 in (0, 7):
            CELLS[x - 1, y1] = first_cells(x, y1)

    def outer(i, carry):
        for x in (0, 3):
            for j in range(2):
                CELLS[x // 2, 2 * i + j] += first_cells(x, 2 * i + j)
        return carry

    lax.fori_loop(0, 4, outer, 0)

    for x1 in range(2):
        parts = split(CELLS[x1].reshape(256, 256), 2)
        pooled = (0.125 * joined(dot(parts, pool_1[...]), 2)).astype(BF16)
        for c in range(3):
            PS[x1 + 1, 1:9, 32 * c : 32 * c + 32] = pooled[:, 128 * c : 128 * c + 128].reshape(
                8, 32, 128
            )

    halo_start(1, pooled_refs)

    load_w2.wait()
    eye = pick(64, 64, lambda r, c: r == c)
    for a in range(3):
        taps_a = w2r[9 * a : 9 * a + 9].reshape(288, 64)
        W2A[64 * (2 - a) : 64 * (2 - a) + 64] = dot_lanes(eye, taps_a).astype(BF16)
        W2B[32 * (2 - a) : 32 * (2 - a) + 32] = jnp.concatenate(
            [w2r[26 - 9 * a - j] for j in range(9)], axis=1
        )
    spread_2 = pick(64, 128, lambda r, c: r == (c >> 1))
    for y2 in range(4):
        SEED[y2] = 0.125 * dot(cot[y2], spread_2)

    def spread_sides(field, ch, xs, ys):
        cells = field[xs, ys, ch : 2 * ch]
        shape = cells.shape
        sides = dot(cells.reshape(-1, 128), shift_2[...]).astype(BF16)
        field[xs, ys, 0:ch] = sides[:, :128].reshape(shape)
        field[xs, ys, 2 * ch :] = sides[:, 128:].reshape(shape)

    def spread_edges(field, ch):
        for x in (0, 3):
            spread_sides(field, ch, x, slice(0, 10))
        for y in (0, 9):
            spread_sides(field, ch, slice(1, 3), y)

    def taps(field, x, y2):
        depth = 3 * field.shape[2]
        one = field[x, pl.ds(2 * y2, 3)].reshape(depth, 128)
        two = field[x, pl.ds(2 * y2 + 1, 3)].reshape(depth, 128)
        return jnp.concatenate([one, two], axis=1)

    def both_rows(field, weights, ch, y2):
        whole = dot(weights[ch : 3 * ch], taps(field, 1, y2))
        whole = whole + dot(weights[0 : 2 * ch], taps(field, 2, y2))
        first = dot(weights[2 * ch : 3 * ch], taps(field, 0, y2))
        last = dot(weights[0:ch], taps(field, 3, y2))
        return whole + jnp.concatenate([first, last], axis=0)

    halo_wait(1, pooled_refs)
    spread_edges(PS, 32)

    def second_block(i, carry):
        for j in range(2):
            y2 = 2 * i + j
            act, slope = act_slope(both_rows(PS, W2A, 64, y2))
            total = act[:64] + act[64:]
            TOT[y2] = total[:, :128] + total[:, 128:]
            seed = jnp.concatenate([SEED[y2]] * 2, axis=0)
            grad = (slope * jnp.concatenate([seed, seed], axis=1)).astype(BF16)
            G2[y2] = grad
            for x1 in range(2):
                for yo in range(2):
                    cells = grad[64 * x1 : 64 * x1 + 64, 128 * yo : 128 * yo + 128]
                    GS[x1 + 1, 2 * y2 + 1 + yo, 64:128] = cells
        return carry

    lax.fori_loop(0, 2, second_block, 0)
    halo_start(2, grad_refs)

    groups = dw2.shape[0]
    share = 64 // groups
    dw2[...] = jnp.zeros_like(dw2)

    def second_grad(y2, carry):
        terms = [None] * 3
        for x in range(4):
            lo, hi = (0 if x < 3 else 64), (128 if x > 0 else 64)
            part = dot_lanes(G2[y2, lo:hi], taps(PS, x, y2))
            for x1 in range(2):
                if 0 <= x - x1 < 3:
                    piece = part[64 * x1 - lo : 64 * x1 - lo + 64]
                    old = terms[x - x1]
                    terms[x - x1] = piece if old is None else old + piece
        for a in range(3):
            for g in range(groups):
                dw2[g, a] += terms[a][share * g : share * g + share]
        return carry

    lax.fori_loop(0, 4, second_grad, 0)
    part2[...] = dw2[...].astype(BF16)

    def group_copies(group, src_of, dst_of, sems, sends=None, gets=None):
        size, me, device = group

        def copy(d, slot):
            peer = lax.rem(me + d, size)
            return pltpu.make_async_remote_copy(
                src_ref=src_of(peer),
                dst_ref=dst_of(peer if slot is None else slot),
                send_sem=sems.at[0, d],
                recv_sem=sems.at[1, peer if slot is None else slot],
                device_id=device(peer),
                device_id_type=MESH,
            )

        def each(allowed, act):
            for d in range(1, size):
                pl.when(allowed(lax.rem(me + d, size)))(functools.partial(act, d))

        def start():
            each(sends, lambda d: copy(d, me).start())

        def wait():
            each(sends, lambda d: copy(d, me).wait_send())
            each(gets, lambda d: copy(d, None).wait_recv())

        return start, wait

    def group_gather(group, slots, sems):
        size, me, device = group

        def start():
            for d in range(1, size):
                pltpu.make_async_remote_copy(
                    src_ref=slots.at[me],
                    dst_ref=slots.at[me],
                    send_sem=sems.at[0],
                    recv_sem=sems.at[1],
                    device_id=device(lax.rem(me + d, size)),
                    device_id_type=MESH,
                ).start()

        def wait():
            others = slots.at[pl.ds(0, size - 1)]
            for sem in (sems.at[0], sems.at[1]):
                pltpu.make_async_copy(others, others, sem).wait()

        return start, wait

    owner = low < 3
    mine = jnp.minimum(low, 2)
    start_a, wait_a = group_copies(
        group_z,
        lambda i: part2.at[lax.rem(i, pencils), jnp.minimum(i // pencils, 2)],
        lambda slot: sum_a.at[slot],
        sem_a,
        sends=lambda i: i // pencils < 3,
        gets=lambda i: owner,
    )
    start_b, wait_b = group_gather(group_xy, sum_b, sem_b)
    start_c, wait_c = group_copies(
        group_low,
        lambda i: sum_c.at[low],
        lambda slot: sum_c.at[slot],
        sem_c,
        sends=lambda i: owner,
        gets=lambda i: i < 3,
    )
    start_z, wait_z = group_gather(group_z, sum_1.at[0], sem_1.at[0])
    start_xy, wait_xy = group_gather(group_xy, sum_1.at[1], sem_1.at[1])

    def total_of(slots, size):
        total = slots[0].astype(F32)
        for i in range(1, size):
            total = total + slots[i].astype(F32)
        return total

    start_a()

    for x in (1, 2):
        spread_sides(GS, 64, x, slice(1, 9))
    pool_2 = pick(128, 64, lambda r, c: (r >> 1) == c)
    pooled = 0.125 * joined(dot(split(TOT[...].reshape(256, 128), 2), pool_2), 2)
    p2_out[...] = pooled.astype(BF16).reshape(4, 64, 64)

    halo_wait(2, grad_refs)
    spread_edges(GS, 64)

    def first_back(i, carry):
        for j in range(2):
            y2 = 2 * i + j
            back = both_rows(GS, W2B, 32, y2)
            for x1 in range(2):
                for yo in range(2):
                    cells = back[32 * x1 : 32 * x1 + 32, 128 * yo : 128 * yo + 128]
                    BACK[x1, 2 * y2 + yo] = cells
        return carry

    lax.fori_loop(0, 2, first_back, 0)
    for x1 in range(2):
        parts = split(BACK[x1].reshape(256, 128), 2)
        CELLS[x1] = (0.125 * joined(dot(parts, spread_1[...]), 2)).reshape(8, 32, 256)

    dw1[...] = jnp.zeros_like(dw1)

    def first_grad(y1, carry):
        total = None
        for x in range(4):
            seed = jnp.concatenate([CELLS[x // 2, y1]] * 2, axis=0)
            term = dot_lanes((SL[x, y1] * seed).astype(BF16), window(x, y1))
            total = term if total is None else total + term
        dw1[...] += total
        return carry

    lax.fori_loop(0, 8, first_grad, 0)

    folded = None
    for yo in range(2):
        term = joined(dot_lanes(split(dw1[32 * yo : 32 * yo + 32], 3), MAPS[yo]), 3)
        folded = term if folded is None else folded + term

    sum_1[0, group_z[1]] = folded.astype(BF16)
    start_z()
    wait_a()

    @pl.when(owner)
    def _():
        sum_a[group_z[1]] = part2[pencil, mine]
        sum_b[group_xy[1]] = total_of(sum_a, group_z[0]).astype(BF16)
        start_b()

    wait_z()
    sum_1[1, group_xy[1]] = total_of(sum_1.at[0], group_z[0]).astype(BF16)
    start_xy()

    @pl.when(owner)
    def _():
        wait_b()
        sum_c[low] = total_of(sum_b, group_xy[0])

    start_c()
    wait_c()
    for a in range(3):
        g2_out[a] = sum_c[a]
    wait_xy()
    g1_out[...] = total_of(sum_1.at[1], group_xy[0])


def solution(mesh):
    pencils = mesh.shape["pencil"]
    share = 64 // pencils
    size_z = LOW * pencils
    size_xy = mesh.shape["slab"] // LOW
    most = max(size_z, size_xy)

    def per_device(volume, weight_one, weight_two, cotangent):
        w1f = jnp.pad(weight_one.reshape(32, 108), ((0, 0), (0, 20)))
        w2 = weight_two.transpose(1, 2, 0)
        cot = cotangent.reshape(64, 4, 64).transpose(1, 0, 2)
        vmem = pl.BlockSpec(memory_space=pltpu.VMEM)
        hbm = pl.BlockSpec(memory_space=pltpu.HBM)
        pooled, grad_one, grad_two = pl.pallas_call(
            kernel,
            out_shape=(
                jax.ShapeDtypeStruct((4, 64, 64), BF16),
                jax.ShapeDtypeStruct((32, 128), F32),
                jax.ShapeDtypeStruct((3, share, 288), F32),
            ),
            in_specs=[hbm, hbm, vmem, vmem],
            out_specs=(vmem,) * 3,
            scratch_shapes=[
                pltpu.VMEM((4, 4, 16, 256), BF16),
                pltpu.VMEM((27, 32, 64), BF16),
                pltpu.VMEM((6, 18, 16, 256), BF16),
                pltpu.VMEM((4, 10, 96, 128), BF16),
                pltpu.VMEM((4, 10, 192, 128), BF16),
                pltpu.VMEM((4, 8, 64, 256), F32),
                pltpu.VMEM((2, 8, 32, 256), F32),
                pltpu.VMEM((4, 64, 128), F32),
                pltpu.VMEM((4, 64, 128), F32),
                pltpu.VMEM((4, 128, 256), BF16),
                pltpu.VMEM((2, 8, 32, 128), F32),
                pltpu.VMEM((192, 288), BF16),
                pltpu.VMEM((96, 576), BF16),
                pltpu.VMEM((2, 128, 192), BF16),
                pltpu.VMEM((256, 384), BF16),
                pltpu.VMEM((128, 256), BF16),
                pltpu.VMEM((128, 256), BF16),
                pltpu.VMEM((2, 16, 256), BF16),
                pltpu.VMEM((2, 4, 16, 256), BF16),
                pltpu.VMEM((2, 16, 256), BF16),
                pltpu.VMEM((4, 16, 256), BF16),
                pltpu.VMEM((64, 192), F32),
                pltpu.VMEM((pencils, 3, share, 288), F32),
                pltpu.VMEM((pencils, 3, share, 288), BF16),
                pltpu.VMEM((size_z, share, 288), BF16),
                pltpu.VMEM((size_xy, share, 288), BF16),
                pltpu.VMEM((LOW, share, 288), F32),
                pltpu.VMEM((2, most, 32, 128), BF16),
                pltpu.SemaphoreType.DMA((2,)),
                pltpu.SemaphoreType.DMA((3, 8)),
                pltpu.SemaphoreType.DMA((3, 8)),
                pltpu.SemaphoreType.DMA((2, size_z)),
                pltpu.SemaphoreType.DMA((2,)),
                pltpu.SemaphoreType.DMA((2, LOW)),
                pltpu.SemaphoreType.DMA((2, 2)),
            ],
            compiler_params=pltpu.CompilerParams(
                collective_id=0, has_side_effects=True, vmem_limit_bytes=40 * 2**20
            ),
        )(volume, w2, w1f, cot)
        pooled_two = pooled.transpose(1, 0, 2).reshape(64, 1, 4, 64)
        grad_one = grad_one[:, :108].reshape(32, 27, 4)
        grad_two = grad_two.transpose(1, 0, 2).reshape(share, 27, 32)
        return (pooled_two, grad_one, grad_two)

    in_specs = (P(None, "slab", "pencil", None), P(), P(), P(None, "slab", "pencil", None))
    out_specs = (P(None, "slab", "pencil", None), P(), P("pencil", None, None))
    return jax.shard_map(
        per_device, mesh=mesh, in_specs=in_specs, out_specs=out_specs, check_vma=False
    )
```

time: 64.7 us -> 54.2 us (0.84)
  Pallas kernels: 58.2 us -> 48 us
    pallas_call x1, Pallas kernels: 58.2 us -> 48 us  [per_device(): pl.pallas_call(kernel, out_shape=(jax.ShapeDtypeStruct((4, 64, 64), BF16)...]
    transpose x2 -> x0, local copies, waits for them, and re-layouts: 1.05 us -> none  [per_device(): w2b = jnp.flip(weight_two, axis=1).transpose(2, 1, 0).reshape(32, 3, 576)]
    reshape x2, local copies, waits for them, and re-layouts: 0.11 us -> 0.85 us  [per_device(): w1f = jnp.pad(weight_one.reshape(32, 108), ((0, 0), (0, 20)))]
    unnamed x11 -> x7, local copies, waits for them, and re-layouts: 3.18 us -> 3.29 us
where the time goes in v3:
time: 54.2 us; the launch traced here: 53.8 us
  Pallas kernels  48 us (89%)
  local copies, waits for them, and re-layouts  5.07 us (9%)
  between operations  0.69 us (1%)
    pallas_call x1, Pallas kernels, per_device(): pl.pallas_call(kernel, out_shape=(jax.ShapeDtypeStruct((4, 64, 64), BF16)...  48 us
    unnamed x7, local copies, waits for them, and re-layouts  3.29 us

profile of v3, /device:TPU:1, one launch (start us, length us, event | category | flops | bytes accessed | tf_op | source)
XLA Modules:
  0.0 53.8 jit_solution(1403635622511540152)
XLA Ops:
  0.6 0.0 copy-start
  0.6 0.9 %copy.18 = bf16[64,1,4,64]{3,0,2,1:T(8,128)(2,1)S(1)} copy(bf16[64,1,4,64]{3,2,1,0:T(4,128)(2,1)} %param.7) | data formatting | bytes 65536 | tf_op args[3]
  1.5 0.8 %reshape.21 = bf16[32,108]{0,1:T(8,128)(2,1)S(1)} reshape(bf16[32,27,4]{0,2,1:T(4,128)(2,1)} %param.5) | data formatting | bytes 13824 | tf_op jit(solution)/shard_map/reshape | solution.py:553
  2.3 0.1 copy.11
  2.4 0.0 copy-done
  2.4 0.0 copy-start.1
  2.4 0.9 %copy-done.1 = bf16[4,4,16,256]{3,2,1,0:T(8,128)(2,1)S(1)} copy-done((bf16[4,4,16,256]{3,2,1,0:T(8,128)(2,1)S(1)}, bf16[4,4,16,256]{3,2,1,0:T(8,128)(2,1)}, u32[]{:S(2)}) %copy-start.1) | copy-done | bytes 131096
  3.3 48.0 %shard_map.67 = (bf16[4,64,64]{2,1,0:T(8,128)(2,1)S(1)}, f32[32,128]{1,0:T(8,128)S(1)}, f32[3,16,288]{2,1,0:T(8,128)S(1)}) custom-call(bf16[4,4,16,256]{3,2,1,0:T(8,128)(2,1)S(1)} %copy-done.1, bf16[27,32,64]{2,1,0:T(8,128)(2,1)S(1)} %bitcast.16, bf16[32,128]{1,0:T(8,128)(2,1)S(1)} %pad.4.w1f, bf16[4,64,64]{2,1,0:T(8,128)(2,1)S(1)} %bitcast.15), custom_call_target="tpu_custom_call" | custom-call | tf_op jit(solution)/shard_map/pallas_call | solution.py:558
  51.4 0.1 reshape.25
  51.5 0.8 %copy.16 = f32[16,27,32]{2,0,1:T(8,128)} copy(f32[16,27,32]{2,1,0:T(8,128)S(1)} %reshape.25) | data formatting | bytes 110592
  52.4 0.1 copy.13
  52.5 0.6 %reshape.24 = f32[32,27,4]{0,2,1:T(4,128)} reshape(f32[32,108]{0,1:T(8,128)S(1)} %copy.13) | data formatting | bytes 27648 | tf_op jit(solution)/shard_map/reshape | solution.py:609
  53.1 0.7 %copy.15 = bf16[64,1,4,64]{3,2,1,0:T(4,128)(2,1)} copy(bf16[64,1,4,64]{3,0,2,1:T(8,128)(2,1)S(1)} %bitcast.18) | data formatting | bytes 65536
  (2 shorter events, 0.0 us)
Async XLA Ops:
  0.6 1.8 %copy-start = (bf16[64,27,32]{0,2,1:T(8,128)(2,1)S(1)}, bf16[64,27,32]{0,2,1:T(8,128)(2,1)}, u32[]{:S(2)}) copy-start(bf16[64,27,32]{0,2,1:T(8,128)(2,1)} %param.6) | copy-start | bytes 331780
  2.4 0.9 %copy-start.1 = (bf16[4,4,16,256]{3,2,1,0:T(8,128)(2,1)S(1)}, bf16[4,4,16,256]{3,2,1,0:T(8,128)(2,1)}, u32[]{:S(2)}) copy-start(bf16[4,4,16,256]{3,2,1,0:T(8,128)(2,1)} %vol_hbm.1) | copy-start | bytes 393220

commit v4 on v3

--- a/solution.py
+++ b/solution.py
@@ -55,21 +55,30 @@
     def hit(r, j):
         b = ((j >> 4) & 3) - yo
         slot = j & 15
-        return (b >= 0) & (b < 3) & (slot < 12) & (r == 36 * (j >> 6) + 12 * b + slot)
-
-    return pick(128, 192, hit)
+        row = 72 * (j >> 6) + 24 * b + 8 * (slot >> 2) + (slot & 3)
+        return (b >= 0) & (b < 3) & (slot < 12) & (r == row)
+
+    return pick(216, 192, hit)
+
+
+def eight_rows(value):
+    value = value.astype(F32)
+    value = jnp.concatenate([value, value], axis=1)
+    return value.reshape(-1, value.shape[2]).astype(BF16)
 
 
 def kernel(
     vol_hbm,
+    w1_hbm,
     w2_hbm,
-    w1f,
-    cot,
+    cot_hbm,
     p2_out,
     g1_out,
     g2_out,
     vol,
+    w1r,
     w2r,
+    cot,
     V,
     PS,
     GS,
@@ -110,9 +119,11 @@
     pencils = lax.axis_size("pencil")
 
     load_vol = pltpu.make_async_copy(vol_hbm, vol, sem_in.at[0])
-    load_w2 = pltpu.make_async_copy(w2_hbm, w2r, sem_in.at[1])
-    load_vol.start()
-    load_w2.start()
+    load_w1 = pltpu.make_async_copy(w1_hbm, w1r, sem_in.at[1])
+    load_w2 = pltpu.make_async_copy(w2_hbm, w2r, sem_in.at[2])
+    load_cot = pltpu.make_async_copy(cot_hbm, cot, sem_in.at[3])
+    for load in (load_vol, load_w1, load_w2, load_cot):
+        load.start()
 
     def exists(dx, dy):
         x = slab + dx
@@ -244,7 +255,10 @@
 
     for yo in range(2):
         MAPS[yo] = expand_map(yo)
-    w1p = jnp.concatenate([dot(w1f[...], MAPS[yo]).astype(BF16) for yo in range(2)], axis=0)
+    load_w1.wait()
+    eye = pick(32, 32, lambda r, c: r == c)
+    w1f = dot_lanes(eye, eight_rows(w1r[...])).astype(BF16)
+    w1p = jnp.concatenate([dot(w1f, MAPS[yo]).astype(BF16) for yo in range(2)], axis=0)
 
     pl.semaphore_wait(barrier, arrivals)
     halo_start(0, volume_refs)
@@ -323,8 +337,10 @@
             [w2r[26 - 9 * a - j] for j in range(9)], axis=1
         )
     spread_2 = pick(64, 128, lambda r, c: r == (c >> 1))
-    for y2 in range(4):
-        SEED[y2] = 0.125 * dot(cot[y2], spread_2)
+    load_cot.wait()
+    to_y2 = pick(256, 512, lambda r, c: c == ((r & 63) << 3) + (r >> 6))
+    seeds = dot(to_y2, eight_rows(cot[...])).astype(BF16)
+    SEED[...] = (0.125 * dot(seeds, spread_2)).reshape(4, 64, 128)
 
     def spread_sides(field, ch, xs, ys):
         cells = field[xs, ys, ch : 2 * ch]
@@ -477,7 +493,9 @@
         spread_sides(GS, 64, x, slice(1, 9))
     pool_2 = pick(128, 64, lambda r, c: (r >> 1) == c)
     pooled = 0.125 * joined(dot(split(TOT[...].reshape(256, 128), 2), pool_2), 2)
-    p2_out[...] = pooled.astype(BF16).reshape(4, 64, 64)
+    from_y2 = pick(512, 256, lambda r, c: r == ((c & 63) << 3) + (c >> 6))
+    pooled = dot(from_y2, pooled.astype(BF16)).reshape(64, 8, 64)
+    p2_out[...] = pooled[:, :4].astype(BF16)
 
     halo_wait(2, grad_refs)
     spread_edges(GS, 64)
@@ -537,9 +555,22 @@
     start_c()
     wait_c()
     for a in range(3):
-        g2_out[a] = sum_c[a]
+        for j in range(9):
+            g2_out[9 * a + j] = sum_c[a, :, 32 * j : 32 * j + 32]
     wait_xy()
-    g1_out[...] = total_of(sum_1.at[1], group_xy[0])
+    total = total_of(sum_1.at[1], group_xy[0]).T
+    for tap in range(27):
+        g1_out[tap] = total[8 * tap : 8 * tap + 4]
+
+
+def write_out(*refs):
+    count = len(refs) // 2
+    sems = refs[-1]
+    copies = [pltpu.make_async_copy(refs[i], refs[count + i], sems.at[i]) for i in range(count)]
+    for copy in copies:
+        copy.start()
+    for copy in copies:
+        copy.wait()
 
 
 def solution(mesh):
@@ -550,23 +581,26 @@
     most = max(size_z, size_xy)
 
     def per_device(volume, weight_one, weight_two, cotangent):
-        w1f = jnp.pad(weight_one.reshape(32, 108), ((0, 0), (0, 20)))
+        w1 = weight_one.transpose(1, 2, 0)
         w2 = weight_two.transpose(1, 2, 0)
-        cot = cotangent.reshape(64, 4, 64).transpose(1, 0, 2)
+        cot = cotangent.reshape(64, 4, 64)
         vmem = pl.BlockSpec(memory_space=pltpu.VMEM)
         hbm = pl.BlockSpec(memory_space=pltpu.HBM)
-        pooled, grad_one, grad_two = pl.pallas_call(
+        shapes = (
+            pltpu.VMEM((64, 4, 64), BF16),
+            pltpu.VMEM((27, 4, 32), F32),
+            pltpu.VMEM((27, share, 32), F32),
+        )
+        results = pl.pallas_call(
             kernel,
-            out_shape=(
-                jax.ShapeDtypeStruct((4, 64, 64), BF16),
-                jax.ShapeDtypeStruct((32, 128), F32),
-                jax.ShapeDtypeStruct((3, share, 288), F32),
-            ),
-            in_specs=[hbm, hbm, vmem, vmem],
+            out_shape=shapes,
+            in_specs=[hbm] * 4,
             out_specs=(vmem,) * 3,
             scratch_shapes=[
                 pltpu.VMEM((4, 4, 16, 256), BF16),
+                pltpu.VMEM((27, 4, 32), BF16),
                 pltpu.VMEM((27, 32, 64), BF16),
+                pltpu.VMEM((64, 4, 64), BF16),
                 pltpu.VMEM((6, 18, 16, 256), BF16),
                 pltpu.VMEM((4, 10, 96, 128), BF16),
                 pltpu.VMEM((4, 10, 192, 128), BF16),
@@ -578,7 +612,7 @@
                 pltpu.VMEM((2, 8, 32, 128), F32),
                 pltpu.VMEM((192, 288), BF16),
                 pltpu.VMEM((96, 576), BF16),
-                pltpu.VMEM((2, 128, 192), BF16),
+                pltpu.VMEM((2, 216, 192), BF16),
                 pltpu.VMEM((256, 384), BF16),
                 pltpu.VMEM((128, 256), BF16),
                 pltpu.VMEM((128, 256), BF16),
@@ -592,8 +626,8 @@
                 pltpu.VMEM((size_z, share, 288), BF16),
                 pltpu.VMEM((size_xy, share, 288), BF16),
                 pltpu.VMEM((LOW, share, 288), F32),
-                pltpu.VMEM((2, most, 32, 128), BF16),
-                pltpu.SemaphoreType.DMA((2,)),
+                pltpu.VMEM((2, most, 32, 216), BF16),
+                pltpu.SemaphoreType.DMA((4,)),
                 pltpu.SemaphoreType.DMA((3, 8)),
                 pltpu.SemaphoreType.DMA((3, 8)),
                 pltpu.SemaphoreType.DMA((2, size_z)),
@@ -602,13 +636,21 @@
                 pltpu.SemaphoreType.DMA((2, 2)),
             ],
             compiler_params=pltpu.CompilerParams(
-                collective_id=0, has_side_effects=True, vmem_limit_bytes=40 * 2**20
+                collective_id=0, has_side_effects=True, vmem_limit_bytes=56 * 2**20
             ),
-        )(volume, w2, w1f, cot)
-        pooled_two = pooled.transpose(1, 0, 2).reshape(64, 1, 4, 64)
-        grad_one = grad_one[:, :108].reshape(32, 27, 4)
-        grad_two = grad_two.transpose(1, 0, 2).reshape(share, 27, 32)
-        return (pooled_two, grad_one, grad_two)
+        )(volume, w1, w2, cot)
+        pooled, grad_one, grad_two = pl.pallas_call(
+            write_out,
+            out_shape=tuple(jax.ShapeDtypeStruct(s.shape, s.dtype) for s in shapes),
+            in_specs=[vmem] * 3,
+            out_specs=(hbm,) * 3,
+            scratch_shapes=[pltpu.SemaphoreType.DMA((3,))],
+        )(*results)
+        return (
+            pooled.reshape(64, 1, 4, 64),
+            grad_one.transpose(2, 0, 1),
+            grad_two.transpose(1, 0, 2),
+        )
 
     in_specs = (P(None, "slab", "pencil", None), P(), P(), P(None, "slab", "pencil", None))
     out_specs = (P(None, "slab", "pencil", None), P(), P("pencil", None, None))

time: 54.2 us -> 54.9 us (1.013)
  Pallas kernels: 48 us -> 51.9 us
  local copies, waits for them, and re-layouts: 5.07 us -> 1.92 us
    pallas_call x1 -> x2, Pallas kernels: 48 us -> 51.9 us  [the longest x1 50.2 us: per_device(): pl.pallas_call(kernel, out_shape=shapes, in_specs=[hbm] * 4, out_specs=(v...]
    reshape x4 -> x0, local copies, waits for them, and re-layouts: 1.62 us -> none  [the longest x2 0.85 us: per_device(): w1f = jnp.pad(weight_one.reshape(32, 108), ((0, 0), (0, 20)))]
    unnamed x7 -> x6, local copies, waits for them, and re-layouts: 3.29 us -> 1.92 us
where the time goes in v4:
time: 54.9 us; the launch traced here: 54.5 us
  Pallas kernels  51.9 us (95%)
  local copies, waits for them, and re-layouts  1.92 us (3%)
  between operations  0.65 us (1%)
    pallas_call x1, Pallas kernels, per_device(): pl.pallas_call(kernel, out_shape=shapes, in_specs=[hbm] * 4, out_specs=(v...  50.2 us
    unnamed x6, local copies, waits for them, and re-layouts  1.92 us
    pallas_call x1, Pallas kernels, per_device(): pl.pallas_call(write_out, out_shape=tuple((jax.ShapeDtypeStruct(s.shape,...  1.75 us

profile of v4, /device:TPU:1, one launch (start us, length us, event | category | flops | bytes accessed | tf_op | source)
XLA Modules:
  0.0 54.5 jit_solution(7201674508243569401)
XLA Ops:
  0.6 50.2 %shard_map.67 = (bf16[64,4,64]{2,1,0:T(4,128)(2,1)S(1)}, f32[27,4,32]{2,1,0:T(4,128)S(1)}, f32[27,16,32]{2,1,0:T(8,128)S(1)}) custom-call(bf16[4,4,16,256]{3,2,1,0:T(8,128)(2,1)} %vol_hbm.1, bf16[27,4,32]{2,1,0:T(4,128)(2,1)} %bitcast.10, bf16[27,32,64]{2,1,0:T(8,128)(2,1)} %bitcast.8, bf16[64,4,64]{2,1,0:T(4,128)(2,1)} %bitcast.9), custom_call_target="tpu_custom_call" | custom-call | tf_op jit(solution)/shard_map/pallas_call | solution.py:594
  50.8 0.0 copy-start
  50.8 0.7 %copy-done = f32[27,16,32]{2,1,0:T(8,128)} copy-done((f32[27,16,32]{2,1,0:T(8,128)}, f32[27,16,32]{2,1,0:T(8,128)S(1)}, u32[]{:S(2)}) %copy-start) | copy-done | bytes 55320
  51.5 0.0 copy-start.1
  51.5 0.6 %copy-done.1 = bf16[64,4,64]{2,1,0:T(4,128)(2,1)} copy-done((bf16[64,4,64]{2,1,0:T(4,128)(2,1)}, bf16[64,4,64]{2,1,0:T(4,128)(2,1)S(1)}, u32[]{:S(2)}) %copy-start.1) | copy-done | bytes 32792
  52.1 0.0 copy-start.2
  52.1 0.6 %copy-done.2 = f32[27,4,32]{2,1,0:T(4,128)} copy-done((f32[27,4,32]{2,1,0:T(4,128)}, f32[27,4,32]{2,1,0:T(4,128)S(1)}, u32[]{:S(2)}) %copy-start.2) | copy-done | bytes 13848
  52.7 1.7 %shard_map.68 = (bf16[64,4,64]{2,1,0:T(4,128)(2,1)}, f32[27,4,32]{2,1,0:T(4,128)}, f32[27,16,32]{2,1,0:T(8,128)}) custom-call(bf16[64,4,64]{2,1,0:T(4,128)(2,1)} %copy-done.1, f32[27,4,32]{2,1,0:T(4,128)} %copy-done.2, f32[27,16,32]{2,1,0:T(8,128)} %copy-done), custom_call_target="tpu_custom_call" | custom-call | tf_op jit(solution)/shard_map/pallas_call | solution.py:642
Async XLA Ops:
  50.8 0.7 %copy-start = (f32[27,16,32]{2,1,0:T(8,128)}, f32[27,16,32]{2,1,0:T(8,128)S(1)}, u32[]{:S(2)}) copy-start(f32[27,16,32]{2,1,0:T(8,128)S(1)} %get-tuple-element.11.refs_2_) | copy-start | bytes 165892
  51.5 0.6 %copy-start.1 = (bf16[64,4,64]{2,1,0:T(4,128)(2,1)}, bf16[64,4,64]{2,1,0:T(4,128)(2,1)S(1)}, u32[]{:S(2)}) copy-start(bf16[64,4,64]{2,1,0:T(4,128)(2,1)S(1)} %get-tuple-element.9.refs_0_) | copy-start | bytes 98308
  52.1 0.6 %copy-start.2 = (f32[27,4,32]{2,1,0:T(4,128)}, f32[27,4,32]{2,1,0:T(4,128)S(1)}, u32[]{:S(2)}) copy-start(f32[27,4,32]{2,1,0:T(4,128)S(1)} %get-tuple-element.10.refs_1_) | copy-start | bytes 41476

commit v5 on v4

--- a/solution.py
+++ b/solution.py
@@ -51,14 +51,14 @@
     return act, 0.65 + 0.35 * t
 
 
-def expand_map(yo):
+def expand_map(yo, rows, slots):
     def hit(r, j):
         b = ((j >> 4) & 3) - yo
         slot = j & 15
-        row = 72 * (j >> 6) + 24 * b + 8 * (slot >> 2) + (slot & 3)
+        row = slots * (9 * (j >> 6) + 3 * b + (slot >> 2)) + (slot & 3)
         return (b >= 0) & (b < 3) & (slot < 12) & (r == row)
 
-    return pick(216, 192, hit)
+    return pick(rows, 192, hit)
 
 
 def eight_rows(value):
@@ -88,6 +88,10 @@
     SEED,
     G2,
     BACK,
+    OUTER,
+    face_x,
+    face_y,
+    corner,
     W2A,
     W2B,
     MAPS,
@@ -173,16 +177,25 @@
             return src, yrecv.at[side]
         return src, crecv.at[2 * (0 if dx == 1 else 1) + side]
 
-    def field_refs(field, lo, hi, dx, dy):
+    def pooled_refs(dx, dy):
         sx = {1: 2, -1: 1, 0: pl.ds(1, 2)}[dx]
         tx = {1: 0, -1: 3, 0: pl.ds(1, 2)}[dx]
         sy = {1: 8, -1: 1, 0: pl.ds(1, 8)}[dy]
         ty = {1: 0, -1: 9, 0: pl.ds(1, 8)}[dy]
-        rows = pl.ds(lo, hi - lo)
-        return field.at[sx, sy, rows], field.at[tx, ty, rows]
-
-    pooled_refs = functools.partial(field_refs, PS, 32, 64)
-    grad_refs = functools.partial(field_refs, GS, 64, 128)
+        rows = pl.ds(32, 32)
+        return PS.at[sx, sy, rows], PS.at[tx, ty, rows]
+
+    def grad_refs(dx, dy):
+        src = OUTER.at[
+            {1: 3, -1: 0, 0: pl.ds(1, 2)}[dx], {1: 9, -1: 0, 0: pl.ds(1, 8)}[dy]
+        ]
+        side_x = 0 if dx == 1 else 1
+        side_y = 0 if dy == 1 else 1
+        if dy == 0:
+            return src, face_x.at[side_x]
+        if dx == 0:
+            return src, face_y.at[side_y]
+        return src, corner.at[2 * side_x + side_y]
 
     for dx, dy in SIDES:
 
@@ -222,6 +235,9 @@
             def _():
                 halo_copy(phase, k, refs).wait_recv()
 
+    for y in (0, 1, 10, 11):
+        GS[:, y] = jnp.zeros((2, 192, 128), BF16)
+
     load_vol.wait()
     edges = pick(32, 256, lambda r, c: c == ((r & 15) << 4) + 15 * (r >> 4))
     packed = dot(edges, vol[...].reshape(256, 256)).astype(BF16)
@@ -253,12 +269,12 @@
         rows = dot(to_rows, rows_of(local, 64 * x, 64 * x + 64)).astype(BF16)
         V[x + 1, 1:17] = rows.reshape(16, 16, 256)
 
-    for yo in range(2):
-        MAPS[yo] = expand_map(yo)
     load_w1.wait()
     eye = pick(32, 32, lambda r, c: r == c)
     w1f = dot_lanes(eye, eight_rows(w1r[...])).astype(BF16)
-    w1p = jnp.concatenate([dot(w1f, MAPS[yo]).astype(BF16) for yo in range(2)], axis=0)
+    w1p = jnp.concatenate(
+        [dot(w1f, expand_map(yo, 216, 8)).astype(BF16) for yo in range(2)], axis=0
+    )
 
     pl.semaphore_wait(barrier, arrivals)
     halo_start(0, volume_refs)
@@ -329,6 +345,8 @@
     halo_start(1, pooled_refs)
 
     load_w2.wait()
+    for yo in range(2):
+        MAPS[yo] = expand_map(yo, 128, 4)
     eye = pick(64, 64, lambda r, c: r == c)
     for a in range(3):
         taps_a = w2r[9 * a : 9 * a + 9].reshape(288, 64)
@@ -342,18 +360,12 @@
     seeds = dot(to_y2, eight_rows(cot[...])).astype(BF16)
     SEED[...] = (0.125 * dot(seeds, spread_2)).reshape(4, 64, 128)
 
-    def spread_sides(field, ch, xs, ys):
-        cells = field[xs, ys, ch : 2 * ch]
+    def spread_edges(xs, ys):
+        cells = PS[xs, ys, 32:64]
         shape = cells.shape
         sides = dot(cells.reshape(-1, 128), shift_2[...]).astype(BF16)
-        field[xs, ys, 0:ch] = sides[:, :128].reshape(shape)
-        field[xs, ys, 2 * ch :] = sides[:, 128:].reshape(shape)
-
-    def spread_edges(field, ch):
-        for x in (0, 3):
-            spread_sides(field, ch, x, slice(0, 10))
-        for y in (0, 9):
-            spread_sides(field, ch, slice(1, 3), y)
+        PS[xs, ys, 0:32] = sides[:, :128].reshape(shape)
+        PS[xs, ys, 64:96] = sides[:, 128:].reshape(shape)
 
     def taps(field, x, y2):
         depth = 3 * field.shape[2]
@@ -361,32 +373,51 @@
         two = field[x, pl.ds(2 * y2 + 1, 3)].reshape(depth, 128)
         return jnp.concatenate([one, two], axis=1)
 
-    def both_rows(field, weights, ch, y2):
-        whole = dot(weights[ch : 3 * ch], taps(field, 1, y2))
-        whole = whole + dot(weights[0 : 2 * ch], taps(field, 2, y2))
-        first = dot(weights[2 * ch : 3 * ch], taps(field, 0, y2))
-        last = dot(weights[0:ch], taps(field, 3, y2))
+    def second_conv(y2):
+        whole = dot(W2A[64:192], taps(PS, 1, y2)) + dot(W2A[0:128], taps(PS, 2, y2))
+        first = dot(W2A[128:192], taps(PS, 0, y2))
+        last = dot(W2A[0:64], taps(PS, 3, y2))
         return whole + jnp.concatenate([first, last], axis=0)
 
     halo_wait(1, pooled_refs)
-    spread_edges(PS, 32)
+    for x in (0, 3):
+        spread_edges(x, slice(0, 10))
+    for y in (0, 9):
+        spread_edges(slice(1, 3), y)
 
     def second_block(i, carry):
         for j in range(2):
             y2 = 2 * i + j
-            act, slope = act_slope(both_rows(PS, W2A, 64, y2))
+            act, slope = act_slope(second_conv(y2))
             total = act[:64] + act[64:]
             TOT[y2] = total[:, :128] + total[:, 128:]
             seed = jnp.concatenate([SEED[y2]] * 2, axis=0)
             grad = (slope * jnp.concatenate([seed, seed], axis=1)).astype(BF16)
             G2[y2] = grad
-            for x1 in range(2):
-                for yo in range(2):
-                    cells = grad[64 * x1 : 64 * x1 + 64, 128 * yo : 128 * yo + 128]
-                    GS[x1 + 1, 2 * y2 + 1 + yo, 64:128] = cells
+            for yo in range(2):
+                cells = grad[:, 128 * yo : 128 * yo + 128]
+                for x1 in range(2):
+                    GS[x1, 2 * y2 + yo + 2, 64:128] = cells[64 * x1 : 64 * x1 + 64]
         return carry
 
     lax.fori_loop(0, 2, second_block, 0)
+    for x1 in range(2):
+        sides = dot(GS[x1, 2:10, 64:128].reshape(512, 128), shift_2[...]).astype(BF16)
+        GS[x1, 2:10, 0:64] = sides[:, :128].reshape(8, 64, 128)
+        GS[x1, 2:10, 128:192] = sides[:, 128:].reshape(8, 64, 128)
+
+    for p in range(5):
+        one = dot(W2B[...], taps(GS, 0, p))
+        two = dot(W2B[...], taps(GS, 1, p))
+        rows = (one[:32], one[32:64] + two[:32], one[64:] + two[32:64], two[64:])
+        for yo in range(2):
+            y = 2 * p + yo
+            for x in range(4):
+                cells = rows[x][:, 128 * yo : 128 * yo + 128]
+                if 0 < x < 3 and 0 < y < 9:
+                    BACK[x - 1, y - 1] = cells
+                else:
+                    OUTER[x, y] = cells.astype(BF16)
     halo_start(2, grad_refs)
 
     groups = dw2.shape[0]
@@ -489,8 +520,6 @@
 
     start_a()
 
-    for x in (1, 2):
-        spread_sides(GS, 64, x, slice(1, 9))
     pool_2 = pick(128, 64, lambda r, c: (r >> 1) == c)
     pooled = 0.125 * joined(dot(split(TOT[...].reshape(256, 128), 2), pool_2), 2)
     from_y2 = pick(512, 256, lambda r, c: r == ((c & 63) << 3) + (c >> 6))
@@ -498,22 +527,13 @@
     p2_out[...] = pooled[:, :4].astype(BF16)
 
     halo_wait(2, grad_refs)
-    spread_edges(GS, 64)
-
-    def first_back(i, carry):
-        for j in range(2):
-            y2 = 2 * i + j
-            back = both_rows(GS, W2B, 32, y2)
-            for x1 in range(2):
-                for yo in range(2):
-                    cells = back[32 * x1 : 32 * x1 + 32, 128 * yo : 128 * yo + 128]
-                    BACK[x1, 2 * y2 + yo] = cells
-        return carry
-
-    lax.fori_loop(0, 2, first_back, 0)
     for x1 in range(2):
-        parts = split(BACK[x1].reshape(256, 128), 2)
-        CELLS[x1] = (0.125 * joined(dot(parts, spread_1[...]), 2)).reshape(8, 32, 256)
+        back = BACK[x1] + face_x[x1].astype(F32)
+        ends = [face_y[i, x1].astype(F32) + corner[2 * x1 + i].astype(F32) for i in range(2)]
+        back = jnp.concatenate(
+            [back[0] + ends[0], back[1:7].reshape(192, 128), back[7] + ends[1]], axis=0
+        )
+        CELLS[x1] = (0.125 * joined(dot(split(back, 2), spread_1[...]), 2)).reshape(8, 32, 256)
 
     dw1[...] = jnp.zeros_like(dw1)
 
@@ -560,7 +580,7 @@
     wait_xy()
     total = total_of(sum_1.at[1], group_xy[0]).T
     for tap in range(27):
-        g1_out[tap] = total[8 * tap : 8 * tap + 4]
+        g1_out[tap] = total[4 * tap : 4 * tap + 4]
 
 
 def write_out(*refs):
@@ -603,16 +623,20 @@
                 pltpu.VMEM((64, 4, 64), BF16),
                 pltpu.VMEM((6, 18, 16, 256), BF16),
                 pltpu.VMEM((4, 10, 96, 128), BF16),
-                pltpu.VMEM((4, 10, 192, 128), BF16),
+                pltpu.VMEM((2, 12, 192, 128), BF16),
                 pltpu.VMEM((4, 8, 64, 256), F32),
                 pltpu.VMEM((2, 8, 32, 256), F32),
                 pltpu.VMEM((4, 64, 128), F32),
                 pltpu.VMEM((4, 64, 128), F32),
                 pltpu.VMEM((4, 128, 256), BF16),
                 pltpu.VMEM((2, 8, 32, 128), F32),
+                pltpu.VMEM((4, 10, 32, 128), BF16),
+                pltpu.VMEM((2, 8, 32, 128), BF16),
+                pltpu.VMEM((2, 2, 32, 128), BF16),
+                pltpu.VMEM((4, 32, 128), BF16),
                 pltpu.VMEM((192, 288), BF16),
                 pltpu.VMEM((96, 576), BF16),
-                pltpu.VMEM((2, 216, 192), BF16),
+                pltpu.VMEM((2, 128, 192), BF16),
                 pltpu.VMEM((256, 384), BF16),
                 pltpu.VMEM((128, 256), BF16),
                 pltpu.VMEM((128, 256), BF16),
@@ -626,7 +650,7 @@
                 pltpu.VMEM((size_z, share, 288), BF16),
                 pltpu.VMEM((size_xy, share, 288), BF16),
                 pltpu.VMEM((LOW, share, 288), F32),
-                pltpu.VMEM((2, most, 32, 216), BF16),
+                pltpu.VMEM((2, most, 32, 128), BF16),
                 pltpu.SemaphoreType.DMA((4,)),
                 pltpu.SemaphoreType.DMA((3, 8)),
                 pltpu.SemaphoreType.DMA((3, 8)),
@@ -645,6 +669,7 @@
             in_specs=[vmem] * 3,
             out_specs=(hbm,) * 3,
             scratch_shapes=[pltpu.SemaphoreType.DMA((3,))],
+            compiler_params=pltpu.CompilerParams(vmem_limit_bytes=4 * 2**20),
         )(*results)
         return (
             pooled.reshape(64, 1, 4, 64),

time: 54.9 us -> 45.6 us (0.83)
  Pallas kernels: 51.9 us -> 44.8 us
  local copies, waits for them, and re-layouts: 1.92 us -> 0 us
    pallas_call x1, Pallas kernels: 50.2 us -> 44.1 us  [per_device(): pl.pallas_call(kernel, out_shape=shapes, in_specs=[hbm] * 4, out_specs=(v...]
    unnamed x6 -> x0, local copies, waits for them, and re-layouts: 1.92 us -> none
    pallas_call x1, Pallas kernels: 1.75 us -> 0.75 us  [per_device(): pl.pallas_call(write_out, out_shape=tuple((jax.ShapeDtypeStruct(s.shape,...]
where the time goes in v5:
time: 45.6 us; the launch traced here: 45.5 us
  Pallas kernels  44.8 us (98%)
  between operations  0.64 us (1%)
    pallas_call x1, Pallas kernels, per_device(): pl.pallas_call(kernel, out_shape=shapes, in_specs=[hbm] * 4, out_specs=(v...  44.1 us

profile of v5, /device:TPU:1, one launch (start us, length us, event | category | flops | bytes accessed | tf_op | source)
XLA Modules:
  0.0 45.5 jit_solution(138555348389809948)
XLA Ops:
  0.6 44.1 %shard_map.67 = (bf16[64,4,64]{2,1,0:T(4,128)(2,1)S(1)}, f32[27,4,32]{2,1,0:T(4,128)S(1)}, f32[27,16,32]{2,1,0:T(8,128)S(1)}) custom-call(bf16[4,4,16,256]{3,2,1,0:T(8,128)(2,1)} %vol_hbm.1, bf16[27,4,32]{2,1,0:T(4,128)(2,1)} %bitcast.10, bf16[27,32,64]{2,1,0:T(8,128)(2,1)} %bitcast.8, bf16[64,4,64]{2,1,0:T(4,128)(2,1)} %bitcast.9), custom_call_target="tpu_custom_call" | custom-call | tf_op jit(solution)/shard_map/pallas_call | solution.py:614
  44.7 0.8 %shard_map.68 = (bf16[64,4,64]{2,1,0:T(4,128)(2,1)}, f32[27,4,32]{2,1,0:T(4,128)}, f32[27,16,32]{2,1,0:T(8,128)}) custom-call(bf16[64,4,64]{2,1,0:T(4,128)(2,1)S(1)} %get-tuple-element.9.refs_0_, f32[27,4,32]{2,1,0:T(4,128)S(1)} %get-tuple-element.10.refs_1_, f32[27,16,32]{2,1,0:T(8,128)S(1)} %get-tuple-element.11.refs_2_), custom_call_target="tpu_custom_call" | custom-call | tf_op jit(solution)/shard_map/pallas_call | solution.py:666

commit v6 on v5

--- a/solution.py
+++ b/solution.py
@@ -12,6 +12,9 @@
 F32 = jnp.float32
 BF16 = jnp.bfloat16
 SIDES = ((1, 1), (1, -1), (-1, 1), (-1, -1), (1, 0), (-1, 0), (0, 1), (0, -1))
+X_FACES = (4, 5)
+OTHERS = (6, 7, 0, 1, 2, 3)
+LOG_2 = 0.6931471805599453
 
 
 def pick(rows, cols, hit):
@@ -45,10 +48,18 @@
     return total
 
 
-def act_slope(pre):
-    t = jnp.tanh(0.5 * pre)
-    act = 0.3 * pre + 0.7 * (jnp.maximum(pre, 0.0) - jnp.log(0.5 + 0.5 * jnp.abs(t)))
+def act_slope(half):
+    t = jnp.tanh(half)
+    act = 1.3 * half + 0.7 * (jnp.abs(half) - jnp.log(1.0 + jnp.abs(t)))
     return act, 0.65 + 0.35 * t
+
+
+def wrap(index, size):
+    return index & (size - 1) if size & (size - 1) == 0 else lax.rem(index, size)
+
+
+def over(index, size):
+    return index >> (size.bit_length() - 1) if size & (size - 1) == 0 else index // size
 
 
 def expand_map(yo, rows, slots):
@@ -140,13 +151,13 @@
             ok = oky if ok is None else ok & oky
         return ok
 
-    low = lax.rem(slab, LOW)
+    low = wrap(slab, LOW)
     group_z = (
         LOW * pencils,
         low * pencils + pencil,
-        lambda i: (slab - low + i // pencils, lax.rem(i, pencils)),
+        lambda i: (slab - low + over(i, pencils), wrap(i, pencils)),
     )
-    group_xy = (slabs // LOW, slab // LOW, lambda i: (i * LOW + low, pencil))
+    group_xy = (slabs // LOW, over(slab, LOW), lambda i: (i * LOW + low, pencil))
     group_low = (LOW, low, lambda i: (slab - low + i, pencil))
 
     barrier = pltpu.get_barrier_semaphore()
@@ -165,7 +176,7 @@
         arrivals = arrivals + (size - 1)
         for d in range(1, size):
             pl.semaphore_signal(
-                barrier, inc=1, device_id=device(lax.rem(me + d, size)), device_id_type=MESH
+                barrier, inc=1, device_id=device(wrap(me + d, size)), device_id_type=MESH
             )
 
     def volume_refs(dx, dy):
@@ -197,21 +208,13 @@
             return src, face_y.at[side_y]
         return src, corner.at[2 * side_x + side_y]
 
-    for dx, dy in SIDES:
-
-        @pl.when(jnp.logical_not(exists(-dx, -dy)))
-        def _():
-            for refs in (volume_refs, pooled_refs, grad_refs):
-                target = refs(dx, dy)[1]
-                target[...] = jnp.zeros(target.shape, BF16)
-
     def halo_copy(phase, k, refs):
         dx, dy = SIDES[k]
         src, dst = refs(dx, dy)
         return pltpu.make_async_remote_copy(
             src_ref=src,
             dst_ref=dst,
-            send_sem=halo_send.at[phase, k],
+            send_sem=halo_send.at[k],
             recv_sem=halo_recv.at[phase, k],
             device_id=(slab + dx, pencil + dy),
             device_id_type=MESH,
@@ -224,8 +227,9 @@
             def _():
                 halo_copy(phase, k, refs).start()
 
-    def halo_wait(phase, refs):
-        for k, (dx, dy) in enumerate(SIDES):
+    def halo_wait(phase, refs, sides):
+        for k in sides:
+            dx, dy = SIDES[k]
 
             @pl.when(exists(dx, dy))
             def _():
@@ -234,15 +238,25 @@
             @pl.when(exists(-dx, -dy))
             def _():
                 halo_copy(phase, k, refs).wait_recv()
-
-    for y in (0, 1, 10, 11):
-        GS[:, y] = jnp.zeros((2, 192, 128), BF16)
 
     load_vol.wait()
     edges = pick(32, 256, lambda r, c: c == ((r & 15) << 4) + 15 * (r >> 4))
     packed = dot(edges, vol[...].reshape(256, 256)).astype(BF16)
     ypack[0] = packed[:16]
     ypack[1] = packed[16:]
+    pl.semaphore_wait(barrier, arrivals)
+    halo_start(0, volume_refs)
+
+    for dx, dy in SIDES:
+
+        @pl.when(jnp.logical_not(exists(-dx, -dy)))
+        def _():
+            for refs in (volume_refs, pooled_refs, grad_refs):
+                target = refs(dx, dy)[1]
+                target[...] = jnp.zeros(target.shape, BF16)
+
+    for y in (0, 1, 10, 11):
+        GS[:, y] = jnp.zeros((2, 192, 128), BF16)
 
     shift_1 = pick(256, 512, lambda r, c: r == jnp.where(c < 256, c - 1, c - 255))
 
@@ -273,11 +287,8 @@
     eye = pick(32, 32, lambda r, c: r == c)
     w1f = dot_lanes(eye, eight_rows(w1r[...])).astype(BF16)
     w1p = jnp.concatenate(
-        [dot(w1f, expand_map(yo, 216, 8)).astype(BF16) for yo in range(2)], axis=0
+        [(0.5 * dot(w1f, expand_map(yo, 216, 8))).astype(BF16) for yo in range(2)], axis=0
     )
-
-    pl.semaphore_wait(barrier, arrivals)
-    halo_start(0, volume_refs)
 
     def window(x, y1):
         return V[pl.ds(x, 3), pl.ds(2 * y1, 4)].reshape(192, 256)
@@ -295,52 +306,50 @@
 
     lax.fori_loop(0, 3, inner, 0)
 
-    def pairs(r, c):
-        return (r >> 1) == (c & 127) + (c >> 7) - 1
-
-    pool_1[...] = pick(256, 384, pairs)
+    pool_1[...] = pick(256, 128, lambda r, c: (r >> 1) == c)
     shift_2[...] = pick(128, 256, lambda r, c: r == jnp.where(c < 128, c - 1, c - 127))
     spread_1[...] = pick(128, 256, lambda r, c: r == (c >> 1))
 
-    halo_wait(0, volume_refs)
-    arrived = shifted(
-        jnp.concatenate(
-            [xrecv[s].reshape(64, 256) for s in range(2)]
-            + [yrecv[s] for s in range(2)]
-            + [crecv[s] for s in range(4)],
-            axis=0,
-        )
-    )
+    def pool_cells(cells):
+        parts = split(cells.reshape(-1, 256), 2)
+        pooled = 0.125 * joined(dot(parts, pool_1[...]), 2) + 0.7 * LOG_2
+        return pooled.astype(BF16).reshape(-1, 32, 128)
+
+    halo_wait(0, volume_refs, X_FACES)
+    arrived = shifted(jnp.concatenate([xrecv[s].reshape(64, 256) for s in range(2)], axis=0))
     for side, x in ((0, 0), (1, 5)):
         rows = dot(to_rows, rows_of(arrived, 64 * side, 64 * side + 64)).astype(BF16)
         V[x, 1:17] = rows.reshape(16, 16, 256)
-    for side, y in ((0, 0), (1, 17)):
-        at = 128 + 16 * side
-        V[1:5, y] = dot(to_edge, rows_of(arrived, at, at + 16)).astype(BF16).reshape(4, 16, 256)
-        at = 160 + 16 * side
-        V[0, y] = dot(to_edge[48:], rows_of(arrived, at, at + 16)).astype(BF16)
-        at = 192 + 16 * side
-        V[5, y] = dot(to_edge[:16], rows_of(arrived, at, at + 16)).astype(BF16)
-
-    for x in (1, 2):
-        for y1 in (0, 7):
-            CELLS[x - 1, y1] = first_cells(x, y1)
 
     def outer(i, carry):
         for x in (0, 3):
-            for j in range(2):
-                CELLS[x // 2, 2 * i + j] += first_cells(x, 2 * i + j)
+            for j in range(3):
+                CELLS[x // 2, 1 + 3 * i + j] += first_cells(x, 1 + 3 * i + j)
         return carry
 
-    lax.fori_loop(0, 4, outer, 0)
-
+    lax.fori_loop(0, 2, outer, 0)
     for x1 in range(2):
-        parts = split(CELLS[x1].reshape(256, 256), 2)
-        pooled = (0.125 * joined(dot(parts, pool_1[...]), 2)).astype(BF16)
-        for c in range(3):
-            PS[x1 + 1, 1:9, 32 * c : 32 * c + 32] = pooled[:, 128 * c : 128 * c + 128].reshape(
-                8, 32, 128
-            )
+        PS[x1 + 1, 2:8, 32:64] = pool_cells(CELLS[x1, 1:7])
+
+    halo_wait(0, volume_refs, OTHERS)
+    arrived = shifted(
+        jnp.concatenate([yrecv[s] for s in range(2)] + [crecv[s] for s in range(4)], axis=0)
+    )
+    for side, y in ((0, 0), (1, 17)):
+        at = 16 * side
+        V[1:5, y] = dot(to_edge, rows_of(arrived, at, at + 16)).astype(BF16).reshape(4, 16, 256)
+        at = 32 + 16 * side
+        V[0, y] = dot(to_edge[48:], rows_of(arrived, at, at + 16)).astype(BF16)
+        at = 64 + 16 * side
+        V[5, y] = dot(to_edge[:16], rows_of(arrived, at, at + 16)).astype(BF16)
+    ends = []
+    for x1 in range(2):
+        for y1 in (0, 7):
+            ends.append(first_cells(2 * x1, y1) + first_cells(2 * x1 + 1, y1))
+    ends = pool_cells(jnp.concatenate(ends, axis=0))
+    for x1 in range(2):
+        PS[x1 + 1, 1, 32:64] = ends[2 * x1]
+        PS[x1 + 1, 8, 32:64] = ends[2 * x1 + 1]
 
     halo_start(1, pooled_refs)
 
@@ -350,7 +359,7 @@
     eye = pick(64, 64, lambda r, c: r == c)
     for a in range(3):
         taps_a = w2r[9 * a : 9 * a + 9].reshape(288, 64)
-        W2A[64 * (2 - a) : 64 * (2 - a) + 64] = dot_lanes(eye, taps_a).astype(BF16)
+        W2A[64 * (2 - a) : 64 * (2 - a) + 64] = (0.5 * dot_lanes(eye, taps_a)).astype(BF16)
         W2B[32 * (2 - a) : 32 * (2 - a) + 32] = jnp.concatenate(
             [w2r[26 - 9 * a - j] for j in range(9)], axis=1
         )
@@ -367,11 +376,14 @@
         PS[xs, ys, 0:32] = sides[:, :128].reshape(shape)
         PS[xs, ys, 64:96] = sides[:, 128:].reshape(shape)
 
-    def taps(field, x, y2):
-        depth = 3 * field.shape[2]
-        one = field[x, pl.ds(2 * y2, 3)].reshape(depth, 128)
-        two = field[x, pl.ds(2 * y2 + 1, 3)].reshape(depth, 128)
+    def taps(field, x, y2, skip=0, count=3):
+        depth = count * field.shape[2]
+        one = field[x, pl.ds(2 * y2 + skip, count)].reshape(depth, 128)
+        two = field[x, pl.ds(2 * y2 + 1 + skip, count)].reshape(depth, 128)
         return jnp.concatenate([one, two], axis=1)
+
+    for x1 in range(2):
+        spread_edges(x1 + 1, slice(1, 9))
 
     def second_conv(y2):
         whole = dot(W2A[64:192], taps(PS, 1, y2)) + dot(W2A[0:128], taps(PS, 2, y2))
@@ -379,15 +391,9 @@
         last = dot(W2A[0:64], taps(PS, 3, y2))
         return whole + jnp.concatenate([first, last], axis=0)
 
-    halo_wait(1, pooled_refs)
-    for x in (0, 3):
-        spread_edges(x, slice(0, 10))
-    for y in (0, 9):
-        spread_edges(slice(1, 3), y)
-
-    def second_block(i, carry):
-        for j in range(2):
-            y2 = 2 * i + j
+
+    def second_block(rows):
+        for y2 in rows:
             act, slope = act_slope(second_conv(y2))
             total = act[:64] + act[64:]
             TOT[y2] = total[:, :128] + total[:, 128:]
@@ -396,19 +402,28 @@
             G2[y2] = grad
             for yo in range(2):
                 cells = grad[:, 128 * yo : 128 * yo + 128]
+                sides = dot(cells, shift_2[...]).astype(BF16)
+                y = 2 * y2 + yo + 2
                 for x1 in range(2):
-                    GS[x1, 2 * y2 + yo + 2, 64:128] = cells[64 * x1 : 64 * x1 + 64]
-        return carry
-
-    lax.fori_loop(0, 2, second_block, 0)
-    for x1 in range(2):
-        sides = dot(GS[x1, 2:10, 64:128].reshape(512, 128), shift_2[...]).astype(BF16)
-        GS[x1, 2:10, 0:64] = sides[:, :128].reshape(8, 64, 128)
-        GS[x1, 2:10, 128:192] = sides[:, 128:].reshape(8, 64, 128)
+                    lo, hi = 64 * x1, 64 * x1 + 64
+                    GS[x1, y, 64:128] = cells[lo:hi]
+                    GS[x1, y, 0:64] = sides[lo:hi, :128]
+                    GS[x1, y, 128:192] = sides[lo:hi, 128:]
+
+    halo_wait(1, pooled_refs, X_FACES)
+    for x in (0, 3):
+        spread_edges(x, slice(1, 9))
+    second_block((1, 2))
+    halo_wait(1, pooled_refs, OTHERS)
+    for y in (0, 9):
+        spread_edges(slice(0, 4), y)
+    second_block((0, 3))
 
     for p in range(5):
-        one = dot(W2B[...], taps(GS, 0, p))
-        two = dot(W2B[...], taps(GS, 1, p))
+        skip, count = (1, 2) if p == 0 else (0, 2) if p == 4 else (0, 3)
+        weights = W2B[:, 192 * skip : 192 * (skip + count)]
+        one = dot(weights, taps(GS, 0, p, skip, count))
+        two = dot(weights, taps(GS, 1, p, skip, count))
         rows = (one[:32], one[32:64] + two[:32], one[64:] + two[32:64], two[64:])
         for yo in range(2):
             y = 2 * p + yo
@@ -442,32 +457,26 @@
     lax.fori_loop(0, 4, second_grad, 0)
     part2[...] = dw2[...].astype(BF16)
 
-    def group_copies(group, src_of, dst_of, sems, sends=None, gets=None):
+    def wait_slots(slots, count, sem):
+        taken = slots.at[pl.ds(0, count)]
+        pltpu.make_async_copy(taken, taken, sem).wait()
+
+    def group_start(group, src_of, dst, sems, sends):
         size, me, device = group
-
-        def copy(d, slot):
-            peer = lax.rem(me + d, size)
-            return pltpu.make_async_remote_copy(
-                src_ref=src_of(peer),
-                dst_ref=dst_of(peer if slot is None else slot),
-                send_sem=sems.at[0, d],
-                recv_sem=sems.at[1, peer if slot is None else slot],
-                device_id=device(peer),
-                device_id_type=MESH,
-            )
-
-        def each(allowed, act):
-            for d in range(1, size):
-                pl.when(allowed(lax.rem(me + d, size)))(functools.partial(act, d))
-
-        def start():
-            each(sends, lambda d: copy(d, me).start())
-
-        def wait():
-            each(sends, lambda d: copy(d, me).wait_send())
-            each(gets, lambda d: copy(d, None).wait_recv())
-
-        return start, wait
+        for d in range(1, size):
+            peer = wrap(me + d, size)
+
+            def start(peer=peer):
+                pltpu.make_async_remote_copy(
+                    src_ref=src_of(peer),
+                    dst_ref=dst.at[me],
+                    send_sem=sems.at[0],
+                    recv_sem=sems.at[1],
+                    device_id=device(peer),
+                    device_id_type=MESH,
+                ).start()
+
+            pl.when(sends(peer))(start)
 
     def group_gather(group, slots, sems):
         size, me, device = group
@@ -479,36 +488,53 @@
                     dst_ref=slots.at[me],
                     send_sem=sems.at[0],
                     recv_sem=sems.at[1],
-                    device_id=device(lax.rem(me + d, size)),
+                    device_id=device(wrap(me + d, size)),
                     device_id_type=MESH,
                 ).start()
 
         def wait():
-            others = slots.at[pl.ds(0, size - 1)]
             for sem in (sems.at[0], sems.at[1]):
-                pltpu.make_async_copy(others, others, sem).wait()
+                wait_slots(slots, size - 1, sem)
 
         return start, wait
 
     owner = low < 3
     mine = jnp.minimum(low, 2)
-    start_a, wait_a = group_copies(
-        group_z,
-        lambda i: part2.at[lax.rem(i, pencils), jnp.minimum(i // pencils, 2)],
-        lambda slot: sum_a.at[slot],
-        sem_a,
-        sends=lambda i: i // pencils < 3,
-        gets=lambda i: owner,
-    )
+
+    def start_a():
+        group_start(
+            group_z,
+            lambda i: part2.at[wrap(i, pencils), jnp.minimum(over(i, pencils), 2)],
+            sum_a,
+            sem_a,
+            lambda i: over(i, pencils) < 3,
+        )
+
+    def wait_a():
+        @pl.when(owner)
+        def _():
+            wait_slots(sum_a, 3 * pencils - 1, sem_a.at[0])
+            wait_slots(sum_a, group_z[0] - 1, sem_a.at[1])
+
+        @pl.when(jnp.logical_not(owner))
+        def _():
+            wait_slots(sum_a, 3 * pencils, sem_a.at[0])
+
     start_b, wait_b = group_gather(group_xy, sum_b, sem_b)
-    start_c, wait_c = group_copies(
-        group_low,
-        lambda i: sum_c.at[low],
-        lambda slot: sum_c.at[slot],
-        sem_c,
-        sends=lambda i: owner,
-        gets=lambda i: i < 3,
-    )
+
+    def start_c():
+        group_start(group_low, lambda i: sum_c.at[low], sum_c, sem_c, lambda i: owner)
+
+    def wait_c():
+        @pl.when(owner)
+        def _():
+            wait_slots(sum_c, LOW - 1, sem_c.at[0])
+            wait_slots(sum_c, 2, sem_c.at[1])
+
+        @pl.when(jnp.logical_not(owner))
+        def _():
+            wait_slots(sum_c, 3, sem_c.at[1])
+
     start_z, wait_z = group_gather(group_z, sum_1.at[0], sem_1.at[0])
     start_xy, wait_xy = group_gather(group_xy, sum_1.at[1], sem_1.at[1])
 
@@ -521,32 +547,47 @@
     start_a()
 
     pool_2 = pick(128, 64, lambda r, c: (r >> 1) == c)
-    pooled = 0.125 * joined(dot(split(TOT[...].reshape(256, 128), 2), pool_2), 2)
+    pooled = 0.125 * joined(dot(split(TOT[...].reshape(256, 128), 2), pool_2), 2) + 0.7 * LOG_2
     from_y2 = pick(512, 256, lambda r, c: r == ((c & 63) << 3) + (c >> 6))
     pooled = dot(from_y2, pooled.astype(BF16)).reshape(64, 8, 64)
     p2_out[...] = pooled[:, :4].astype(BF16)
 
-    halo_wait(2, grad_refs)
-    for x1 in range(2):
-        back = BACK[x1] + face_x[x1].astype(F32)
-        ends = [face_y[i, x1].astype(F32) + corner[2 * x1 + i].astype(F32) for i in range(2)]
-        back = jnp.concatenate(
-            [back[0] + ends[0], back[1:7].reshape(192, 128), back[7] + ends[1]], axis=0
-        )
-        CELLS[x1] = (0.125 * joined(dot(split(back, 2), spread_1[...]), 2)).reshape(8, 32, 256)
-
-    dw1[...] = jnp.zeros_like(dw1)
-
-    def first_grad(y1, carry):
+    def spread_back(back):
+        cells = split(back.reshape(-1, 128), 2)
+        return (0.125 * joined(dot(cells, spread_1[...]), 2)).reshape(-1, 32, 256)
+
+    def first_grad(y1, seeds):
         total = None
         for x in range(4):
-            seed = jnp.concatenate([CELLS[x // 2, y1]] * 2, axis=0)
+            seed = jnp.concatenate([seeds[x // 2]] * 2, axis=0)
             term = dot_lanes((SL[x, y1] * seed).astype(BF16), window(x, y1))
+            total = term if total is None else total + term
+        return total
+
+    halo_wait(2, grad_refs, X_FACES)
+    for x1 in range(2):
+        CELLS[x1] = spread_back(BACK[x1] + face_x[x1].astype(F32))
+    dw1[...] = jnp.zeros_like(dw1)
+
+    def middle(i, carry):
+        total = None
+        for j in range(3):
+            y1 = 1 + 3 * i + j
+            term = first_grad(y1, (CELLS[0, y1], CELLS[1, y1]))
             total = term if total is None else total + term
         dw1[...] += total
         return carry
 
-    lax.fori_loop(0, 8, first_grad, 0)
+    lax.fori_loop(0, 2, middle, 0)
+
+    halo_wait(2, grad_refs, OTHERS)
+    for side, y1 in ((0, 0), (1, 7)):
+        back = []
+        for x1 in range(2):
+            own = BACK[x1, y1] + face_x[x1, y1].astype(F32)
+            back.append(own + face_y[side, x1].astype(F32) + corner[2 * x1 + side].astype(F32))
+        seeds = spread_back(jnp.concatenate(back, axis=0))
+        dw1[...] += first_grad(y1, (seeds[0], seeds[1]))
 
     folded = None
     for yo in range(2):
@@ -637,7 +678,7 @@
                 pltpu.VMEM((192, 288), BF16),
                 pltpu.VMEM((96, 576), BF16),
                 pltpu.VMEM((2, 128, 192), BF16),
-                pltpu.VMEM((256, 384), BF16),
+                pltpu.VMEM((256, 128), BF16),
                 pltpu.VMEM((128, 256), BF16),
                 pltpu.VMEM((128, 256), BF16),
                 pltpu.VMEM((2, 16, 256), BF16),
@@ -652,11 +693,11 @@
                 pltpu.VMEM((LOW, share, 288), F32),
                 pltpu.VMEM((2, most, 32, 128), BF16),
                 pltpu.SemaphoreType.DMA((4,)),
+                pltpu.SemaphoreType.DMA((8,)),
                 pltpu.SemaphoreType.DMA((3, 8)),
-                pltpu.SemaphoreType.DMA((3, 8)),
-                pltpu.SemaphoreType.DMA((2, size_z)),
                 pltpu.SemaphoreType.DMA((2,)),
-                pltpu.SemaphoreType.DMA((2, LOW)),
+                pltpu.SemaphoreType.DMA((2,)),
+                pltpu.SemaphoreType.DMA((2,)),
                 pltpu.SemaphoreType.DMA((2, 2)),
             ],
             compiler_params=pltpu.CompilerParams(

time: 45.6 us -> 43.5 us (0.954)
  Pallas kernels: 44.8 us -> 42.7 us
    pallas_call x1, Pallas kernels: 44.1 us -> 42 us  [per_device(): pl.pallas_call(kernel, out_shape=shapes, in_specs=[hbm] * 4, out_specs=(v...]
where the time goes in v6:
time: 43.5 us; the launch traced here: 43.4 us
  Pallas kernels  42.7 us (98%)
  between operations  0.64 us (1%)
    pallas_call x1, Pallas kernels, per_device(): pl.pallas_call(kernel, out_shape=shapes, in_specs=[hbm] * 4, out_specs=(v...  42 us

profile of v6, /device:TPU:1, one launch (start us, length us, event | category | flops | bytes accessed | tf_op | source)
XLA Modules:
  0.0 43.4 jit_solution(17331260575822040804)
XLA Ops:
  0.6 42.0 %shard_map.67 = (bf16[64,4,64]{2,1,0:T(4,128)(2,1)S(1)}, f32[27,4,32]{2,1,0:T(4,128)S(1)}, f32[27,16,32]{2,1,0:T(8,128)S(1)}) custom-call(bf16[4,4,16,256]{3,2,1,0:T(8,128)(2,1)} %vol_hbm.1, bf16[27,4,32]{2,1,0:T(4,128)(2,1)} %bitcast.10, bf16[27,32,64]{2,1,0:T(8,128)(2,1)} %bitcast.8, bf16[64,4,64]{2,1,0:T(4,128)(2,1)} %bitcast.9), custom_call_target="tpu_custom_call" | custom-call | tf_op jit(solution)/shard_map/pallas_call | solution.py:655
  42.6 0.8 %shard_map.68 = (bf16[64,4,64]{2,1,0:T(4,128)(2,1)}, f32[27,4,32]{2,1,0:T(4,128)}, f32[27,16,32]{2,1,0:T(8,128)}) custom-call(bf16[64,4,64]{2,1,0:T(4,128)(2,1)S(1)} %get-tuple-element.9.refs_0_, f32[27,4,32]{2,1,0:T(4,128)S(1)} %get-tuple-element.10.refs_1_, f32[27,16,32]{2,1,0:T(8,128)S(1)} %get-tuple-element.11.refs_2_), custom_call_target="tpu_custom_call" | custom-call | tf_op jit(solution)/shard_map/pallas_call | solution.py:707

commit v7 on v6

--- a/solution.py
+++ b/solution.py
@@ -49,9 +49,12 @@
 
 
 def act_slope(half):
+    rows = half.shape[0] // 2
     t = jnp.tanh(half)
-    act = 1.3 * half + 0.7 * (jnp.abs(half) - jnp.log(1.0 + jnp.abs(t)))
-    return act, 0.65 + 0.35 * t
+    size = jnp.abs(half)
+    grown = 1.0 + jnp.abs(t)
+    size = size[:rows] + size[rows:] - jnp.log(grown[:rows] * grown[rows:])
+    return 1.3 * (half[:rows] + half[rows:]) + 0.7 * size, 0.65 + 0.35 * t
 
 
 def wrap(index, size):
@@ -98,6 +101,7 @@
     TOT,
     SEED,
     G2,
+    LOCAL,
     BACK,
     OUTER,
     face_x,
@@ -296,7 +300,7 @@
     def first_cells(x, y1):
         act, slope = act_slope(dot(w1p, window(x, y1)))
         SL[x, y1] = slope
-        return act[:32] + act[32:]
+        return act
 
     def inner(i, carry):
         for x in (1, 2):
@@ -385,17 +389,21 @@
     for x1 in range(2):
         spread_edges(x1 + 1, slice(1, 9))
 
-    def second_conv(y2):
-        whole = dot(W2A[64:192], taps(PS, 1, y2)) + dot(W2A[0:128], taps(PS, 2, y2))
+    def local_conv(y2):
+        return dot(W2A[64:192], taps(PS, 1, y2)) + dot(W2A[0:128], taps(PS, 2, y2))
+
+    def second_conv(y2, local):
         first = dot(W2A[128:192], taps(PS, 0, y2))
         last = dot(W2A[0:64], taps(PS, 3, y2))
-        return whole + jnp.concatenate([first, last], axis=0)
-
+        return local + jnp.concatenate([first, last], axis=0)
+
+    for y2 in (1, 2):
+        LOCAL[y2 - 1] = local_conv(y2)
 
     def second_block(rows):
         for y2 in rows:
-            act, slope = act_slope(second_conv(y2))
-            total = act[:64] + act[64:]
+            local = LOCAL[y2 - 1] if y2 in (1, 2) else local_conv(y2)
+            total, slope = act_slope(second_conv(y2, local))
             TOT[y2] = total[:, :128] + total[:, 128:]
             seed = jnp.concatenate([SEED[y2]] * 2, axis=0)
             grad = (slope * jnp.concatenate([seed, seed], axis=1)).astype(BF16)
@@ -410,16 +418,7 @@
                     GS[x1, y, 0:64] = sides[lo:hi, :128]
                     GS[x1, y, 128:192] = sides[lo:hi, 128:]
 
-    halo_wait(1, pooled_refs, X_FACES)
-    for x in (0, 3):
-        spread_edges(x, slice(1, 9))
-    second_block((1, 2))
-    halo_wait(1, pooled_refs, OTHERS)
-    for y in (0, 9):
-        spread_edges(slice(0, 4), y)
-    second_block((0, 3))
-
-    for p in range(5):
+    def gradient_halo(p):
         skip, count = (1, 2) if p == 0 else (0, 2) if p == 4 else (0, 3)
         weights = W2B[:, 192 * skip : 192 * (skip + count)]
         one = dot(weights, taps(GS, 0, p, skip, count))
@@ -433,10 +432,22 @@
                     BACK[x - 1, y - 1] = cells
                 else:
                     OUTER[x, y] = cells.astype(BF16)
+
+    halo_wait(1, pooled_refs, X_FACES)
+    for x in (0, 3):
+        spread_edges(x, slice(1, 9))
+    second_block((1, 2))
+    gradient_halo(2)
+    halo_wait(1, pooled_refs, OTHERS)
+    for y in (0, 9):
+        spread_edges(slice(0, 4), y)
+    second_block((0, 3))
+
+    for p in (0, 1, 3, 4):
+        gradient_halo(p)
     halo_start(2, grad_refs)
 
-    groups = dw2.shape[0]
-    share = 64 // groups
+    share = 64 // pencils
     dw2[...] = jnp.zeros_like(dw2)
 
     def second_grad(y2, carry):
@@ -450,93 +461,50 @@
                     old = terms[x - x1]
                     terms[x - x1] = piece if old is None else old + piece
         for a in range(3):
-            for g in range(groups):
-                dw2[g, a] += terms[a][share * g : share * g + share]
+            dw2[a] += terms[a]
         return carry
 
     lax.fori_loop(0, 4, second_grad, 0)
-    part2[...] = dw2[...].astype(BF16)
+    columns = [dw2[a] for a in range(3)] + [jnp.zeros((64, 256 * LOW - 864), F32)]
+    columns = jnp.concatenate(columns, axis=1).astype(BF16)
+    for g in range(pencils):
+        for part in range(LOW):
+            rows = columns[share * g : share * g + share]
+            part2[g, part] = rows[:, 256 * part : 256 * part + 256]
 
     def wait_slots(slots, count, sem):
         taken = slots.at[pl.ds(0, count)]
         pltpu.make_async_copy(taken, taken, sem).wait()
 
-    def group_start(group, src_of, dst, sems, sends):
+    def group_copies(group, slots, sems, src_of=None):
         size, me, device = group
-        for d in range(1, size):
-            peer = wrap(me + d, size)
-
-            def start(peer=peer):
+
+        def start():
+            for d in range(1, size):
+                peer = wrap(me + d, size)
                 pltpu.make_async_remote_copy(
-                    src_ref=src_of(peer),
-                    dst_ref=dst.at[me],
+                    src_ref=slots.at[me] if src_of is None else src_of(peer),
+                    dst_ref=slots.at[me],
                     send_sem=sems.at[0],
                     recv_sem=sems.at[1],
                     device_id=device(peer),
                     device_id_type=MESH,
                 ).start()
 
-            pl.when(sends(peer))(start)
-
-    def group_gather(group, slots, sems):
-        size, me, device = group
-
-        def start():
-            for d in range(1, size):
-                pltpu.make_async_remote_copy(
-                    src_ref=slots.at[me],
-                    dst_ref=slots.at[me],
-                    send_sem=sems.at[0],
-                    recv_sem=sems.at[1],
-                    device_id=device(wrap(me + d, size)),
-                    device_id_type=MESH,
-                ).start()
-
         def wait():
             for sem in (sems.at[0], sems.at[1]):
                 wait_slots(slots, size - 1, sem)
 
         return start, wait
 
-    owner = low < 3
-    mine = jnp.minimum(low, 2)
-
-    def start_a():
-        group_start(
-            group_z,
-            lambda i: part2.at[wrap(i, pencils), jnp.minimum(over(i, pencils), 2)],
-            sum_a,
-            sem_a,
-            lambda i: over(i, pencils) < 3,
-        )
-
-    def wait_a():
-        @pl.when(owner)
-        def _():
-            wait_slots(sum_a, 3 * pencils - 1, sem_a.at[0])
-            wait_slots(sum_a, group_z[0] - 1, sem_a.at[1])
-
-        @pl.when(jnp.logical_not(owner))
-        def _():
-            wait_slots(sum_a, 3 * pencils, sem_a.at[0])
-
-    start_b, wait_b = group_gather(group_xy, sum_b, sem_b)
-
-    def start_c():
-        group_start(group_low, lambda i: sum_c.at[low], sum_c, sem_c, lambda i: owner)
-
-    def wait_c():
-        @pl.when(owner)
-        def _():
-            wait_slots(sum_c, LOW - 1, sem_c.at[0])
-            wait_slots(sum_c, 2, sem_c.at[1])
-
-        @pl.when(jnp.logical_not(owner))
-        def _():
-            wait_slots(sum_c, 3, sem_c.at[1])
-
-    start_z, wait_z = group_gather(group_z, sum_1.at[0], sem_1.at[0])
-    start_xy, wait_xy = group_gather(group_xy, sum_1.at[1], sem_1.at[1])
+    def part_of(i):
+        return part2.at[wrap(i, pencils), over(i, pencils)]
+
+    start_a, wait_a = group_copies(group_z, sum_a, sem_a, part_of)
+    start_b, wait_b = group_copies(group_xy, sum_b, sem_b)
+    start_c, wait_c = group_copies(group_low, sum_c, sem_c)
+    start_z, wait_z = group_copies(group_z, sum_1.at[0], sem_1.at[0])
+    start_xy, wait_xy = group_copies(group_xy, sum_1.at[1], sem_1.at[1])
 
     def total_of(slots, size):
         total = slots[0].astype(F32)
@@ -597,27 +565,19 @@
     sum_1[0, group_z[1]] = folded.astype(BF16)
     start_z()
     wait_a()
-
-    @pl.when(owner)
-    def _():
-        sum_a[group_z[1]] = part2[pencil, mine]
-        sum_b[group_xy[1]] = total_of(sum_a, group_z[0]).astype(BF16)
-        start_b()
-
+    sum_a[group_z[1]] = part2[pencil, low]
+    sum_b[group_xy[1]] = total_of(sum_a, group_z[0]).astype(BF16)
+    start_b()
     wait_z()
     sum_1[1, group_xy[1]] = total_of(sum_1.at[0], group_z[0]).astype(BF16)
     start_xy()
-
-    @pl.when(owner)
-    def _():
-        wait_b()
-        sum_c[low] = total_of(sum_b, group_xy[0])
-
+    wait_b()
+    sum_c[low] = total_of(sum_b, group_xy[0])
     start_c()
     wait_c()
-    for a in range(3):
-        for j in range(9):
-            g2_out[9 * a + j] = sum_c[a, :, 32 * j : 32 * j + 32]
+    for tap in range(27):
+        at = 32 * (tap % 8)
+        g2_out[tap] = sum_c[tap // 8, :, at : at + 32]
     wait_xy()
     total = total_of(sum_1.at[1], group_xy[0]).T
     for tap in range(27):
@@ -670,6 +630,7 @@
                 pltpu.VMEM((4, 64, 128), F32),
                 pltpu.VMEM((4, 64, 128), F32),
                 pltpu.VMEM((4, 128, 256), BF16),
+                pltpu.VMEM((2, 128, 256), F32),
                 pltpu.VMEM((2, 8, 32, 128), F32),
                 pltpu.VMEM((4, 10, 32, 128), BF16),
                 pltpu.VMEM((2, 8, 32, 128), BF16),
@@ -686,11 +647,11 @@
                 pltpu.VMEM((2, 16, 256), BF16),
                 pltpu.VMEM((4, 16, 256), BF16),
                 pltpu.VMEM((64, 192), F32),
-                pltpu.VMEM((pencils, 3, share, 288), F32),
-                pltpu.VMEM((pencils, 3, share, 288), BF16),
-                pltpu.VMEM((size_z, share, 288), BF16),
-                pltpu.VMEM((size_xy, share, 288), BF16),
-                pltpu.VMEM((LOW, share, 288), F32),
+                pltpu.VMEM((3, 64, 288), F32),
+                pltpu.VMEM((pencils, LOW, share, 256), BF16),
+                pltpu.VMEM((size_z, share, 256), BF16),
+                pltpu.VMEM((size_xy, share, 256), BF16),
+                pltpu.VMEM((LOW, share, 256), F32),
                 pltpu.VMEM((2, most, 32, 128), BF16),
                 pltpu.SemaphoreType.DMA((4,)),
                 pltpu.SemaphoreType.DMA((8,)),

time: 43.5 us -> 42.8 us (0.984)
  Pallas kernels: 42.7 us -> 42.1 us
    pallas_call x1, Pallas kernels: 42 us -> 41.3 us  [per_device(): pl.pallas_call(kernel, out_shape=shapes, in_specs=[hbm] * 4, out_specs=(v...]
where the time goes in v7:
time: 42.8 us; the launch traced here: 42.7 us
  Pallas kernels  42.1 us (98%)
  between operations  0.64 us (1%)
    pallas_call x1, Pallas kernels, per_device(): pl.pallas_call(kernel, out_shape=shapes, in_specs=[hbm] * 4, out_specs=(v...  41.3 us

profile of v7, /device:TPU:1, one launch (start us, length us, event | category | flops | bytes accessed | tf_op | source)
XLA Modules:
  0.0 42.7 jit_solution(2743943706129964149)
XLA Ops:
  0.6 41.3 %shard_map.67 = (bf16[64,4,64]{2,1,0:T(4,128)(2,1)S(1)}, f32[27,4,32]{2,1,0:T(4,128)S(1)}, f32[27,16,32]{2,1,0:T(8,128)S(1)}) custom-call(bf16[4,4,16,256]{3,2,1,0:T(8,128)(2,1)} %vol_hbm.1, bf16[27,4,32]{2,1,0:T(4,128)(2,1)} %bitcast.10, bf16[27,32,64]{2,1,0:T(8,128)(2,1)} %bitcast.8, bf16[64,4,64]{2,1,0:T(4,128)(2,1)} %bitcast.9), custom_call_target="tpu_custom_call" | custom-call | tf_op jit(solution)/shard_map/pallas_call | solution.py:615
  42.0 0.8 %shard_map.68 = (bf16[64,4,64]{2,1,0:T(4,128)(2,1)}, f32[27,4,32]{2,1,0:T(4,128)}, f32[27,16,32]{2,1,0:T(8,128)}) custom-call(bf16[64,4,64]{2,1,0:T(4,128)(2,1)S(1)} %get-tuple-element.9.refs_0_, f32[27,4,32]{2,1,0:T(4,128)S(1)} %get-tuple-element.10.refs_1_, f32[27,16,32]{2,1,0:T(8,128)S(1)} %get-tuple-element.11.refs_2_), custom_call_target="tpu_custom_call" | custom-call | tf_op jit(solution)/shard_map/pallas_call | solution.py:668

commit v8 on v7

--- a/solution.py
+++ b/solution.py
@@ -14,6 +14,7 @@
 SIDES = ((1, 1), (1, -1), (-1, 1), (-1, -1), (1, 0), (-1, 0), (0, 1), (0, -1))
 X_FACES = (4, 5)
 OTHERS = (6, 7, 0, 1, 2, 3)
+ALL = tuple(range(8))
 LOG_2 = 0.6931471805599453
 
 
@@ -192,13 +193,17 @@
             return src, yrecv.at[side]
         return src, crecv.at[2 * (0 if dx == 1 else 1) + side]
 
-    def pooled_refs(dx, dy):
+    def pooled_refs(dx, dy, ys=pl.ds(1, 8)):
         sx = {1: 2, -1: 1, 0: pl.ds(1, 2)}[dx]
         tx = {1: 0, -1: 3, 0: pl.ds(1, 2)}[dx]
-        sy = {1: 8, -1: 1, 0: pl.ds(1, 8)}[dy]
-        ty = {1: 0, -1: 9, 0: pl.ds(1, 8)}[dy]
+        sy = {1: 8, -1: 1, 0: ys}[dy]
+        ty = {1: 0, -1: 9, 0: ys}[dy]
         rows = pl.ds(32, 32)
         return PS.at[sx, sy, rows], PS.at[tx, ty, rows]
+
+    middle_refs = functools.partial(pooled_refs, ys=pl.ds(2, 6))
+    low_refs = functools.partial(pooled_refs, ys=1)
+    high_refs = functools.partial(pooled_refs, ys=8)
 
     def grad_refs(dx, dy):
         src = OUTER.at[
@@ -215,19 +220,20 @@
     def halo_copy(phase, k, refs):
         dx, dy = SIDES[k]
         src, dst = refs(dx, dy)
+        extra = 2 * (phase - 3) + k - 4
         return pltpu.make_async_remote_copy(
             src_ref=src,
             dst_ref=dst,
-            send_sem=halo_send.at[k],
-            recv_sem=halo_recv.at[phase, k],
+            send_sem=halo_send.at[k if phase < 3 else 8 + extra],
+            recv_sem=halo_recv.at[8 * phase + k if phase < 3 else 24 + extra],
             device_id=(slab + dx, pencil + dy),
             device_id_type=MESH,
         )
 
-    def halo_start(phase, refs):
-        for k, (dx, dy) in enumerate(SIDES):
-
-            @pl.when(exists(dx, dy))
+    def halo_start(phase, refs, sides):
+        for k in sides:
+
+            @pl.when(exists(*SIDES[k]))
             def _():
                 halo_copy(phase, k, refs).start()
 
@@ -249,7 +255,7 @@
     ypack[0] = packed[:16]
     ypack[1] = packed[16:]
     pl.semaphore_wait(barrier, arrivals)
-    halo_start(0, volume_refs)
+    halo_start(0, volume_refs, ALL)
 
     for dx, dy in SIDES:
 
@@ -258,9 +264,6 @@
             for refs in (volume_refs, pooled_refs, grad_refs):
                 target = refs(dx, dy)[1]
                 target[...] = jnp.zeros(target.shape, BF16)
-
-    for y in (0, 1, 10, 11):
-        GS[:, y] = jnp.zeros((2, 192, 128), BF16)
 
     shift_1 = pick(256, 512, lambda r, c: r == jnp.where(c < 256, c - 1, c - 255))
 
@@ -334,6 +337,7 @@
     lax.fori_loop(0, 2, outer, 0)
     for x1 in range(2):
         PS[x1 + 1, 2:8, 32:64] = pool_cells(CELLS[x1, 1:7])
+    halo_start(3, middle_refs, X_FACES)
 
     halo_wait(0, volume_refs, OTHERS)
     arrived = shifted(
@@ -355,7 +359,9 @@
         PS[x1 + 1, 1, 32:64] = ends[2 * x1]
         PS[x1 + 1, 8, 32:64] = ends[2 * x1 + 1]
 
-    halo_start(1, pooled_refs)
+    halo_start(1, pooled_refs, OTHERS)
+    halo_start(1, low_refs, X_FACES)
+    halo_start(4, high_refs, X_FACES)
 
     load_w2.wait()
     for yo in range(2):
@@ -364,9 +370,10 @@
     for a in range(3):
         taps_a = w2r[9 * a : 9 * a + 9].reshape(288, 64)
         W2A[64 * (2 - a) : 64 * (2 - a) + 64] = (0.5 * dot_lanes(eye, taps_a)).astype(BF16)
-        W2B[32 * (2 - a) : 32 * (2 - a) + 32] = jnp.concatenate(
-            [w2r[26 - 9 * a - j] for j in range(9)], axis=1
-        )
+        for b in range(3):
+            at = 32 * (3 * b + a)
+            taps_b = [w2r[26 - 9 * a - 3 * b - c] for c in range(3)]
+            W2B[at : at + 32] = jnp.concatenate(taps_b, axis=1)
     spread_2 = pick(64, 128, lambda r, c: r == (c >> 1))
     load_cot.wait()
     to_y2 = pick(256, 512, lambda r, c: c == ((r & 63) << 3) + (r >> 6))
@@ -380,21 +387,20 @@
         PS[xs, ys, 0:32] = sides[:, :128].reshape(shape)
         PS[xs, ys, 64:96] = sides[:, 128:].reshape(shape)
 
-    def taps(field, x, y2, skip=0, count=3):
-        depth = count * field.shape[2]
-        one = field[x, pl.ds(2 * y2 + skip, count)].reshape(depth, 128)
-        two = field[x, pl.ds(2 * y2 + 1 + skip, count)].reshape(depth, 128)
+    def taps(x, y2):
+        one = PS[x, pl.ds(2 * y2, 3)].reshape(288, 128)
+        two = PS[x, pl.ds(2 * y2 + 1, 3)].reshape(288, 128)
         return jnp.concatenate([one, two], axis=1)
 
     for x1 in range(2):
         spread_edges(x1 + 1, slice(1, 9))
 
     def local_conv(y2):
-        return dot(W2A[64:192], taps(PS, 1, y2)) + dot(W2A[0:128], taps(PS, 2, y2))
+        return dot(W2A[64:192], taps(1, y2)) + dot(W2A[0:128], taps(2, y2))
 
     def second_conv(y2, local):
-        first = dot(W2A[128:192], taps(PS, 0, y2))
-        last = dot(W2A[0:64], taps(PS, 3, y2))
+        first = dot(W2A[128:192], taps(0, y2))
+        last = dot(W2A[0:64], taps(3, y2))
         return local + jnp.concatenate([first, last], axis=0)
 
     for y2 in (1, 2):
@@ -411,60 +417,72 @@
             for yo in range(2):
                 cells = grad[:, 128 * yo : 128 * yo + 128]
                 sides = dot(cells, shift_2[...]).astype(BF16)
-                y = 2 * y2 + yo + 2
+                y = 2 * y2 + yo
                 for x1 in range(2):
                     lo, hi = 64 * x1, 64 * x1 + 64
                     GS[x1, y, 64:128] = cells[lo:hi]
                     GS[x1, y, 0:64] = sides[lo:hi, :128]
                     GS[x1, y, 128:192] = sides[lo:hi, 128:]
 
-    def gradient_halo(p):
-        skip, count = (1, 2) if p == 0 else (0, 2) if p == 4 else (0, 3)
-        weights = W2B[:, 192 * skip : 192 * (skip + count)]
-        one = dot(weights, taps(GS, 0, p, skip, count))
-        two = dot(weights, taps(GS, 1, p, skip, count))
-        rows = (one[:32], one[32:64] + two[:32], one[64:] + two[32:64], two[64:])
-        for yo in range(2):
-            y = 2 * p + yo
-            for x in range(4):
-                cells = rows[x][:, 128 * yo : 128 * yo + 128]
-                if 0 < x < 3 and 0 < y < 9:
-                    BACK[x - 1, y - 1] = cells
-                else:
-                    OUTER[x, y] = cells.astype(BF16)
-
-    halo_wait(1, pooled_refs, X_FACES)
+    def back_terms(y2):
+        given = {}
+        for x1 in range(2):
+            cells = jnp.concatenate([GS[x1, 2 * y2], GS[x1, 2 * y2 + 1]], axis=1)
+            terms = dot(W2B[...], cells)
+            for b in range(3):
+                for a in range(3):
+                    at = 32 * (3 * b + a)
+                    for yo in range(2):
+                        term = terms[at : at + 32, 128 * yo : 128 * yo + 128]
+                        place = (x1 + 2 - a, 2 * y2 + yo + 2 - b)
+                        given[place] = given[place] + term if place in given else term
+        for (x, y), term in given.items():
+            met = {1: (), 2: (4, 5), 0: (2, 3), 3: (6, 7)}[y2]
+            BACK[x, y] = BACK[x, y] + term if y in met else term
+
+    halo_wait(3, middle_refs, X_FACES)
     for x in (0, 3):
-        spread_edges(x, slice(1, 9))
+        spread_edges(x, slice(2, 8))
     second_block((1, 2))
-    gradient_halo(2)
+    back_terms(1)
+    back_terms(2)
     halo_wait(1, pooled_refs, OTHERS)
+    halo_wait(1, low_refs, X_FACES)
+    halo_wait(4, high_refs, X_FACES)
     for y in (0, 9):
         spread_edges(slice(0, 4), y)
+    for x in (0, 3):
+        for y in (1, 8):
+            spread_edges(x, y)
     second_block((0, 3))
-
-    for p in (0, 1, 3, 4):
-        gradient_halo(p)
-    halo_start(2, grad_refs)
+    back_terms(0)
+    back_terms(3)
+    for x in (0, 3):
+        OUTER[x] = BACK[x].astype(BF16)
+    for y in (0, 9):
+        OUTER[1:3, y] = BACK[1:3, y].astype(BF16)
+
+    halo_start(2, grad_refs, ALL)
 
     share = 64 // pencils
     dw2[...] = jnp.zeros_like(dw2)
 
-    def second_grad(y2, carry):
+    def second_grad(i, carry):
         terms = [None] * 3
-        for x in range(4):
-            lo, hi = (0 if x < 3 else 64), (128 if x > 0 else 64)
-            part = dot_lanes(G2[y2, lo:hi], taps(PS, x, y2))
-            for x1 in range(2):
-                if 0 <= x - x1 < 3:
-                    piece = part[64 * x1 - lo : 64 * x1 - lo + 64]
-                    old = terms[x - x1]
-                    terms[x - x1] = piece if old is None else old + piece
+        for y2 in (2 * i, 2 * i + 1):
+            for x in range(4):
+                lo, hi = (0 if x < 3 else 64), (128 if x > 0 else 64)
+                part = dot_lanes(G2[y2, lo:hi], taps(x, y2))
+                for x1 in range(2):
+                    if 0 <= x - x1 < 3:
+                        piece = part[64 * x1 - lo : 64 * x1 - lo + 64]
+                        old = terms[x - x1]
+                        terms[x - x1] = piece if old is None else old + piece
         for a in range(3):
             dw2[a] += terms[a]
         return carry
 
-    lax.fori_loop(0, 4, second_grad, 0)
+    lax.fori_loop(0, 2, second_grad, 0)
     columns = [dw2[a] for a in range(3)] + [jnp.zeros((64, 256 * LOW - 864), F32)]
     columns = jnp.concatenate(columns, axis=1).astype(BF16)
     for g in range(pencils):
@@ -534,7 +552,7 @@
 
     halo_wait(2, grad_refs, X_FACES)
     for x1 in range(2):
-        CELLS[x1] = spread_back(BACK[x1] + face_x[x1].astype(F32))
+        CELLS[x1] = spread_back(BACK[x1 + 1, 1:9] + face_x[x1].astype(F32))
     dw1[...] = jnp.zeros_like(dw1)
 
     def middle(i, carry):
@@ -552,7 +570,7 @@
     for side, y1 in ((0, 0), (1, 7)):
         back = []
         for x1 in range(2):
-            own = BACK[x1, y1] + face_x[x1, y1].astype(F32)
+            own = BACK[x1 + 1, y1 + 1] + face_x[x1, y1].astype(F32)
             back.append(own + face_y[side, x1].astype(F32) + corner[2 * x1 + side].astype(F32))
         seeds = spread_back(jnp.concatenate(back, axis=0))
         dw1[...] += first_grad(y1, (seeds[0], seeds[1]))
@@ -624,20 +642,20 @@
                 pltpu.VMEM((64, 4, 64), BF16),
                 pltpu.VMEM((6, 18, 16, 256), BF16),
                 pltpu.VMEM((4, 10, 96, 128), BF16),
-                pltpu.VMEM((2, 12, 192, 128), BF16),
+                pltpu.VMEM((2, 8, 192, 128), BF16),
                 pltpu.VMEM((4, 8, 64, 256), F32),
                 pltpu.VMEM((2, 8, 32, 256), F32),
                 pltpu.VMEM((4, 64, 128), F32),
                 pltpu.VMEM((4, 64, 128), F32),
                 pltpu.VMEM((4, 128, 256), BF16),
                 pltpu.VMEM((2, 128, 256), F32),
-                pltpu.VMEM((2, 8, 32, 128), F32),
+                pltpu.VMEM((4, 10, 32, 128), F32),
                 pltpu.VMEM((4, 10, 32, 128), BF16),
                 pltpu.VMEM((2, 8, 32, 128), BF16),
                 pltpu.VMEM((2, 2, 32, 128), BF16),
                 pltpu.VMEM((4, 32, 128), BF16),
                 pltpu.VMEM((192, 288), BF16),
-                pltpu.VMEM((96, 576), BF16),
+                pltpu.VMEM((288, 192), BF16),
                 pltpu.VMEM((2, 128, 192), BF16),
                 pltpu.VMEM((256, 128), BF16),
                 pltpu.VMEM((128, 256), BF16),
@@ -654,8 +672,8 @@
                 pltpu.VMEM((LOW, share, 256), F32),
                 pltpu.VMEM((2, most, 32, 128), BF16),
                 pltpu.SemaphoreType.DMA((4,)),
-                pltpu.SemaphoreType.DMA((8,)),
-                pltpu.SemaphoreType.DMA((3, 8)),
+                pltpu.SemaphoreType.DMA((12,)),
+                pltpu.SemaphoreType.DMA((28,)),
                 pltpu.SemaphoreType.DMA((2,)),
                 pltpu.SemaphoreType.DMA((2,)),
                 pltpu.SemaphoreType.DMA((2,)),

time: 42.8 us -> 43 us (level)
  no operation moved by 1% of the time
where the time goes in v8:
time: 43 us; the launch traced here: 42.9 us
  Pallas kernels  42.3 us (98%)
  between operations  0.64 us (1%)
    pallas_call x1, Pallas kernels, per_device(): pl.pallas_call(kernel, out_shape=shapes, in_specs=[hbm] * 4, out_specs=(v...  41.5 us

profile of v8, /device:TPU:1, one launch (start us, length us, event | category | flops | bytes accessed | tf_op | source)
XLA Modules:
  0.0 42.9 jit_solution(596538972918850934)
XLA Ops:
  0.6 41.5 %shard_map.67 = (bf16[64,4,64]{2,1,0:T(4,128)(2,1)S(1)}, f32[27,4,32]{2,1,0:T(4,128)S(1)}, f32[27,16,32]{2,1,0:T(8,128)S(1)}) custom-call(bf16[4,4,16,256]{3,2,1,0:T(8,128)(2,1)} %vol_hbm.1, bf16[27,4,32]{2,1,0:T(4,128)(2,1)} %bitcast.10, bf16[27,32,64]{2,1,0:T(8,128)(2,1)} %bitcast.8, bf16[64,4,64]{2,1,0:T(4,128)(2,1)} %bitcast.9), custom_call_target="tpu_custom_call" | custom-call | tf_op jit(solution)/shard_map/pallas_call | solution.py:633
  42.2 0.8 %shard_map.68 = (bf16[64,4,64]{2,1,0:T(4,128)(2,1)}, f32[27,4,32]{2,1,0:T(4,128)}, f32[27,16,32]{2,1,0:T(8,128)}) custom-call(bf16[64,4,64]{2,1,0:T(4,128)(2,1)S(1)} %get-tuple-element.9.refs_0_, f32[27,4,32]{2,1,0:T(4,128)S(1)} %get-tuple-element.10.refs_1_, f32[27,16,32]{2,1,0:T(8,128)S(1)} %get-tuple-element.11.refs_2_), custom_call_target="tpu_custom_call" | custom-call | tf_op jit(solution)/shard_map/pallas_call | solution.py:686

commit v9 on v8

--- a/solution.py
+++ b/solution.py
@@ -13,7 +13,7 @@
 BF16 = jnp.bfloat16
 SIDES = ((1, 1), (1, -1), (-1, 1), (-1, -1), (1, 0), (-1, 0), (0, 1), (0, -1))
 X_FACES = (4, 5)
-OTHERS = (6, 7, 0, 1, 2, 3)
+OTHERS = (0, 1, 2, 3, 6, 7)
 ALL = tuple(range(8))
 LOG_2 = 0.6931471805599453
 
@@ -165,6 +165,23 @@
     group_xy = (slabs // LOW, over(slab, LOW), lambda i: (i * LOW + low, pencil))
     group_low = (LOW, low, lambda i: (slab - low + i, pencil))
 
+    def others(group):
+        size, me, _ = group
+        if group is group_xy and size == 16:
+            steps = [(dx, dy) for dx in range(4) for dy in range(4) if dx or dy]
+            steps.sort(key=lambda step: -sum(min(d, 4 - d) for d in step))
+            return [((me + 4 * dx) & 12) + ((me + dy) & 3) for dx, dy in steps]
+        if group is group_z and size == 16:
+            z = 2 * pencil + (low >> 1)
+            steps = [(dz, core) for dz in range(8) for core in range(2) if dz or core]
+            steps.sort(key=lambda step: -min(step[0], 8 - step[0]))
+            found = []
+            for dz, core in steps:
+                there = (z + dz) & 7
+                found.append(8 * (there & 1) + 4 * ((low + core) & 1) + (there >> 1))
+            return found
+        return [wrap(me + d, size) for d in range(1, size)]
+
     barrier = pltpu.get_barrier_semaphore()
     arrivals = 0
     for dx, dy in SIDES:
@@ -177,11 +194,11 @@
                 barrier, inc=1, device_id=(slab + dx, pencil + dy), device_id_type=MESH
             )
 
-    for size, me, device in (group_z, group_xy):
-        arrivals = arrivals + (size - 1)
-        for d in range(1, size):
+    for group in (group_z, group_xy):
+        arrivals = arrivals + (group[0] - 1)
+        for peer in others(group):
             pl.semaphore_signal(
-                barrier, inc=1, device_id=device(wrap(me + d, size)), device_id_type=MESH
+                barrier, inc=1, device_id=group[2](peer), device_id_type=MESH
             )
 
     def volume_refs(dx, dy):
@@ -440,12 +457,27 @@
             met = {1: (), 2: (4, 5), 0: (2, 3), 3: (6, 7)}[y2]
             BACK[x, y] = BACK[x, y] + term if y in met else term
 
+    def second_grad(rows):
+        terms = [None] * 3
+        for y2 in rows:
+            for x in range(4):
+                lo, hi = (0 if x < 3 else 64), (128 if x > 0 else 64)
+                part = dot_lanes(G2[y2, lo:hi], taps(x, y2))
+                for x1 in range(2):
+                    if 0 <= x - x1 < 3:
+                        piece = part[64 * x1 - lo : 64 * x1 - lo + 64]
+                        old = terms[x - x1]
+                        terms[x - x1] = piece if old is None else old + piece
+        for a in range(3):
+            dw2[rows[0], a] = terms[a]
+
     halo_wait(3, middle_refs, X_FACES)
     for x in (0, 3):
         spread_edges(x, slice(2, 8))
     second_block((1, 2))
     back_terms(1)
     back_terms(2)
+    second_grad((1, 2))
     halo_wait(1, pooled_refs, OTHERS)
     halo_wait(1, low_refs, X_FACES)
     halo_wait(4, high_refs, X_FACES)
@@ -465,25 +497,8 @@
     halo_start(2, grad_refs, ALL)
 
     share = 64 // pencils
-    dw2[...] = jnp.zeros_like(dw2)
-
-    def second_grad(i, carry):
-        terms = [None] * 3
-        for y2 in (2 * i, 2 * i + 1):
-            for x in range(4):
-                lo, hi = (0 if x < 3 else 64), (128 if x > 0 else 64)
-                part = dot_lanes(G2[y2, lo:hi], taps(x, y2))
-                for x1 in range(2):
-                    if 0 <= x - x1 < 3:
-                        piece = part[64 * x1 - lo : 64 * x1 - lo + 64]
-                        old = terms[x - x1]
-                        terms[x - x1] = piece if old is None else old + piece
-        for a in range(3):
-            dw2[a] += terms[a]
-        return carry
-
-    lax.fori_loop(0, 2, second_grad, 0)
-    columns = [dw2[a] for a in range(3)] + [jnp.zeros((64, 256 * LOW - 864), F32)]
+    second_grad((0, 3))
+    columns = [dw2[0, a] + dw2[1, a] for a in range(3)] + [jnp.zeros((64, 256 * LOW - 864), F32)]
     columns = jnp.concatenate(columns, axis=1).astype(BF16)
     for g in range(pencils):
         for part in range(LOW):
@@ -498,8 +513,7 @@
         size, me, device = group
 
         def start():
-            for d in range(1, size):
-                peer = wrap(me + d, size)
+            for peer in others(group):
                 pltpu.make_async_remote_copy(
                     src_ref=slots.at[me] if src_of is None else src_of(peer),
                     dst_ref=slots.at[me],
@@ -590,16 +604,17 @@
     sum_1[1, group_xy[1]] = total_of(sum_1.at[0], group_z[0]).astype(BF16)
     start_xy()
     wait_b()
-    sum_c[low] = total_of(sum_b, group_xy[0])
+    sum_c[low] = total_of(sum_b, group_xy[0]).astype(BF16)
     start_c()
-    wait_c()
-    for tap in range(27):
-        at = 32 * (tap % 8)
-        g2_out[tap] = sum_c[tap // 8, :, at : at + 32]
     wait_xy()
     total = total_of(sum_1.at[1], group_xy[0]).T
     for tap in range(27):
         g1_out[tap] = total[4 * tap : 4 * tap + 4]
+    wait_c()
+    totals = [sum_c[i].astype(F32) for i in range(LOW)]
+    for tap in range(27):
+        at = 32 * (tap % 8)
+        g2_out[tap] = totals[tap // 8][:, at : at + 32]
 
 
 def write_out(*refs):
@@ -665,11 +680,11 @@
                 pltpu.VMEM((2, 16, 256), BF16),
                 pltpu.VMEM((4, 16, 256), BF16),
                 pltpu.VMEM((64, 192), F32),
-                pltpu.VMEM((3, 64, 288), F32),
+                pltpu.VMEM((2, 3, 64, 288), F32),
                 pltpu.VMEM((pencils, LOW, share, 256), BF16),
                 pltpu.VMEM((size_z, share, 256), BF16),
                 pltpu.VMEM((size_xy, share, 256), BF16),
-                pltpu.VMEM((LOW, share, 256), F32),
+                pltpu.VMEM((LOW, share, 256), BF16),
                 pltpu.VMEM((2, most, 32, 128), BF16),
                 pltpu.SemaphoreType.DMA((4,)),
                 pltpu.SemaphoreType.DMA((12,)),

time: 43 us -> 42.2 us (0.981)
  Pallas kernels: 42.3 us -> 41.5 us
    pallas_call x1, Pallas kernels: 41.5 us -> 40.7 us  [per_device(): pl.pallas_call(kernel, out_shape=shapes, in_specs=[hbm] * 4, out_specs=(v...]
where the time goes in v9:
time: 42.2 us; the launch traced here: 42.1 us
  Pallas kernels  41.5 us (98%)
  between operations  0.64 us (2%)
    pallas_call x1, Pallas kernels, per_device(): pl.pallas_call(kernel, out_shape=shapes, in_specs=[hbm] * 4, out_specs=(v...  40.7 us

profile of v9, /device:TPU:1, one launch (start us, length us, event | category | flops | bytes accessed | tf_op | source)
XLA Modules:
  0.0 42.1 jit_solution(12532574511965933614)
XLA Ops:
  0.6 40.7 %shard_map.67 = (bf16[64,4,64]{2,1,0:T(4,128)(2,1)S(1)}, f32[27,4,32]{2,1,0:T(4,128)S(1)}, f32[27,16,32]{2,1,0:T(8,128)S(1)}) custom-call(bf16[4,4,16,256]{3,2,1,0:T(8,128)(2,1)} %vol_hbm.1, bf16[27,4,32]{2,1,0:T(4,128)(2,1)} %bitcast.10, bf16[27,32,64]{2,1,0:T(8,128)(2,1)} %bitcast.8, bf16[64,4,64]{2,1,0:T(4,128)(2,1)} %bitcast.9), custom_call_target="tpu_custom_call" | custom-call | tf_op jit(solution)/shard_map/pallas_call | solution.py:648
  41.4 0.8 %shard_map.68 = (bf16[64,4,64]{2,1,0:T(4,128)(2,1)}, f32[27,4,32]{2,1,0:T(4,128)}, f32[27,16,32]{2,1,0:T(8,128)}) custom-call(bf16[64,4,64]{2,1,0:T(4,128)(2,1)S(1)} %get-tuple-element.9.refs_0_, f32[27,4,32]{2,1,0:T(4,128)S(1)} %get-tuple-element.10.refs_1_, f32[27,16,32]{2,1,0:T(8,128)S(1)} %get-tuple-element.11.refs_2_), custom_call_target="tpu_custom_call" | custom-call | tf_op jit(solution)/shard_map/pallas_call | solution.py:701

commit v10 on v9

--- a/solution.py
+++ b/solution.py
@@ -351,7 +351,8 @@
                 CELLS[x // 2, 1 + 3 * i + j] += first_cells(x, 1 + 3 * i + j)
         return carry
 
-    lax.fori_loop(0, 2, outer, 0)
+    for i in range(2):
+        outer(i, 0)
     for x1 in range(2):
         PS[x1 + 1, 2:8, 32:64] = pool_cells(CELLS[x1, 1:7])
     halo_start(3, middle_refs, X_FACES)
@@ -578,7 +579,8 @@
         dw1[...] += total
         return carry
 
-    lax.fori_loop(0, 2, middle, 0)
+    for i in range(2):
+        middle(i, 0)
 
     halo_wait(2, grad_refs, OTHERS)
     for side, y1 in ((0, 0), (1, 7)):

time: 42.2 us -> 41.6 us (0.986)
  Pallas kernels: 41.5 us -> 40.9 us
    pallas_call x1, Pallas kernels: 40.7 us -> 40.2 us  [per_device(): pl.pallas_call(kernel, out_shape=shapes, in_specs=[hbm] * 4, out_specs=(v...]
where the time goes in v10:
time: 41.6 us
  Pallas kernels  40.9 us (98%)
  between operations  0.64 us (2%)
    pallas_call x1, Pallas kernels, per_device(): pl.pallas_call(kernel, out_shape=shapes, in_specs=[hbm] * 4, out_specs=(v...  40.2 us

profile of v10, /device:TPU:1, one launch (start us, length us, event | category | flops | bytes accessed | tf_op | source)
XLA Modules:
  0.0 41.6 jit_solution(554285736403127426)
XLA Ops:
  0.6 40.2 %shard_map.67 = (bf16[64,4,64]{2,1,0:T(4,128)(2,1)S(1)}, f32[27,4,32]{2,1,0:T(4,128)S(1)}, f32[27,16,32]{2,1,0:T(8,128)S(1)}) custom-call(bf16[4,4,16,256]{3,2,1,0:T(8,128)(2,1)} %vol_hbm.1, bf16[27,4,32]{2,1,0:T(4,128)(2,1)} %bitcast.10, bf16[27,32,64]{2,1,0:T(8,128)(2,1)} %bitcast.8, bf16[64,4,64]{2,1,0:T(4,128)(2,1)} %bitcast.9), custom_call_target="tpu_custom_call" | custom-call | tf_op jit(solution)/shard_map/pallas_call | solution.py:650
  40.8 0.8 %shard_map.68 = (bf16[64,4,64]{2,1,0:T(4,128)(2,1)}, f32[27,4,32]{2,1,0:T(4,128)}, f32[27,16,32]{2,1,0:T(8,128)}) custom-call(bf16[64,4,64]{2,1,0:T(4,128)(2,1)S(1)} %get-tuple-element.9.refs_0_, f32[27,4,32]{2,1,0:T(4,128)S(1)} %get-tuple-element.10.refs_1_, f32[27,16,32]{2,1,0:T(8,128)S(1)} %get-tuple-element.11.refs_2_), custom_call_target="tpu_custom_call" | custom-call | tf_op jit(solution)/shard_map/pallas_call | solution.py:703

commit v11 on v10

--- a/solution.py
+++ b/solution.py
@@ -242,7 +242,7 @@
             src_ref=src,
             dst_ref=dst,
             send_sem=halo_send.at[k if phase < 3 else 8 + extra],
-            recv_sem=halo_recv.at[8 * phase + k if phase < 3 else 24 + extra],
+            recv_sem=halo_recv.at[8 * (phase % 2) + k if phase < 3 else 16 + extra],
             device_id=(slab + dx, pencil + dy),
             device_id_type=MESH,
         )
@@ -690,7 +690,7 @@
                 pltpu.VMEM((2, most, 32, 128), BF16),
                 pltpu.SemaphoreType.DMA((4,)),
                 pltpu.SemaphoreType.DMA((12,)),
-                pltpu.SemaphoreType.DMA((28,)),
+                pltpu.SemaphoreType.DMA((20,)),
                 pltpu.SemaphoreType.DMA((2,)),
                 pltpu.SemaphoreType.DMA((2,)),
                 pltpu.SemaphoreType.DMA((2,)),

time: 41.6 us -> 41.6 us (level)
  no operation moved by 1% of the time
where the time goes in v11:
time: 41.6 us; the launch traced here: 41.5 us
  Pallas kernels  40.8 us (98%)
  between operations  0.64 us (2%)
    pallas_call x1, Pallas kernels, per_device(): pl.pallas_call(kernel, out_shape=shapes, in_specs=[hbm] * 4, out_specs=(v...  40.1 us

profile of v11, /device:TPU:1, one launch (start us, length us, event | category | flops | bytes accessed | tf_op | source)
XLA Modules:
  0.0 41.5 jit_solution(3157702131236851796)
XLA Ops:
  0.6 40.1 %shard_map.67 = (bf16[64,4,64]{2,1,0:T(4,128)(2,1)S(1)}, f32[27,4,32]{2,1,0:T(4,128)S(1)}, f32[27,16,32]{2,1,0:T(8,128)S(1)}) custom-call(bf16[4,4,16,256]{3,2,1,0:T(8,128)(2,1)} %vol_hbm.1, bf16[27,4,32]{2,1,0:T(4,128)(2,1)} %bitcast.10, bf16[27,32,64]{2,1,0:T(8,128)(2,1)} %bitcast.8, bf16[64,4,64]{2,1,0:T(4,128)(2,1)} %bitcast.9), custom_call_target="tpu_custom_call" | custom-call | tf_op jit(solution)/shard_map/pallas_call | solution.py:650
  40.7 0.8 %shard_map.68 = (bf16[64,4,64]{2,1,0:T(4,128)(2,1)}, f32[27,4,32]{2,1,0:T(4,128)}, f32[27,16,32]{2,1,0:T(8,128)}) custom-call(bf16[64,4,64]{2,1,0:T(4,128)(2,1)S(1)} %get-tuple-element.9.refs_0_, f32[27,4,32]{2,1,0:T(4,128)S(1)} %get-tuple-element.10.refs_1_, f32[27,16,32]{2,1,0:T(8,128)S(1)} %get-tuple-element.11.refs_2_), custom_call_target="tpu_custom_call" | custom-call | tf_op jit(solution)/shard_map/pallas_call | solution.py:703

commit v12 on v11

--- a/solution.py
+++ b/solution.py
@@ -510,7 +510,7 @@
         taken = slots.at[pl.ds(0, count)]
         pltpu.make_async_copy(taken, taken, sem).wait()
 
-    def group_copies(group, slots, sems, src_of=None):
+    def group_copies(group, slots, send, recv, src_of=None):
         size, me, device = group
 
         def start():
@@ -518,14 +518,14 @@
                 pltpu.make_async_remote_copy(
                     src_ref=slots.at[me] if src_of is None else src_of(peer),
                     dst_ref=slots.at[me],
-                    send_sem=sems.at[0],
-                    recv_sem=sems.at[1],
+                    send_sem=send,
+                    recv_sem=recv,
                     device_id=device(peer),
                     device_id_type=MESH,
                 ).start()
 
         def wait():
-            for sem in (sems.at[0], sems.at[1]):
+            for sem in (send, recv):
                 wait_slots(slots, size - 1, sem)
 
         return start, wait
@@ -533,11 +533,11 @@
     def part_of(i):
         return part2.at[wrap(i, pencils), over(i, pencils)]
 
-    start_a, wait_a = group_copies(group_z, sum_a, sem_a, part_of)
-    start_b, wait_b = group_copies(group_xy, sum_b, sem_b)
-    start_c, wait_c = group_copies(group_low, sum_c, sem_c)
-    start_z, wait_z = group_copies(group_z, sum_1.at[0], sem_1.at[0])
-    start_xy, wait_xy = group_copies(group_xy, sum_1.at[1], sem_1.at[1])
+    start_a, wait_a = group_copies(group_z, sum_a, sem_a.at[0], sem_a.at[1], part_of)
+    start_b, wait_b = group_copies(group_xy, sum_b, sem_a.at[0], sem_b.at[0])
+    start_c, wait_c = group_copies(group_low, sum_c, sem_a.at[0], sem_c.at[0])
+    start_z, wait_z = group_copies(group_z, sum_1.at[0], sem_1.at[0], sem_1.at[1])
+    start_xy, wait_xy = group_copies(group_xy, sum_1.at[1], sem_1.at[0], sem_1.at[2])
 
     def total_of(slots, size):
         total = slots[0].astype(F32)
@@ -692,9 +692,9 @@
                 pltpu.SemaphoreType.DMA((12,)),
                 pltpu.SemaphoreType.DMA((20,)),
                 pltpu.SemaphoreType.DMA((2,)),
-                pltpu.SemaphoreType.DMA((2,)),
-                pltpu.SemaphoreType.DMA((2,)),
-                pltpu.SemaphoreType.DMA((2, 2)),
+                pltpu.SemaphoreType.DMA((1,)),
+                pltpu.SemaphoreType.DMA((1,)),
+                pltpu.SemaphoreType.DMA((3,)),
             ],
             compiler_params=pltpu.CompilerParams(
                 collective_id=0, has_side_effects=True, vmem_limit_bytes=56 * 2**20

time: 41.6 us -> 41.6 us (level)
  no operation moved by 1% of the time
where the time goes in v12:
time: 41.6 us; the launch traced here: 41.5 us
  Pallas kernels  40.8 us (98%)
  between operations  0.64 us (2%)
    pallas_call x1, Pallas kernels, per_device(): pl.pallas_call(kernel, out_shape=shapes, in_specs=[hbm] * 4, out_specs=(v...  40.1 us

profile of v12, /device:TPU:1, one launch (start us, length us, event | category | flops | bytes accessed | tf_op | source)
XLA Modules:
  0.0 41.5 jit_solution(1720511125884630341)
XLA Ops:
  0.6 40.1 %shard_map.67 = (bf16[64,4,64]{2,1,0:T(4,128)(2,1)S(1)}, f32[27,4,32]{2,1,0:T(4,128)S(1)}, f32[27,16,32]{2,1,0:T(8,128)S(1)}) custom-call(bf16[4,4,16,256]{3,2,1,0:T(8,128)(2,1)} %vol_hbm.1, bf16[27,4,32]{2,1,0:T(4,128)(2,1)} %bitcast.10, bf16[27,32,64]{2,1,0:T(8,128)(2,1)} %bitcast.8, bf16[64,4,64]{2,1,0:T(4,128)(2,1)} %bitcast.9), custom_call_target="tpu_custom_call" | custom-call | tf_op jit(solution)/shard_map/pallas_call | solution.py:650
  40.7 0.8 %shard_map.68 = (bf16[64,4,64]{2,1,0:T(4,128)(2,1)}, f32[27,4,32]{2,1,0:T(4,128)}, f32[27,16,32]{2,1,0:T(8,128)}) custom-call(bf16[64,4,64]{2,1,0:T(4,128)(2,1)S(1)} %get-tuple-element.9.refs_0_, f32[27,4,32]{2,1,0:T(4,128)S(1)} %get-tuple-element.10.refs_1_, f32[27,16,32]{2,1,0:T(8,128)S(1)} %get-tuple-element.11.refs_2_), custom_call_target="tpu_custom_call" | custom-call | tf_op jit(solution)/shard_map/pallas_call | solution.py:703
